TPU v7x, 32 devices: a whole 2x2x4 slice. The times are simulated.
32 devices in a mesh: gx: 4 (over y, x), gy: 4 (over z), dst: 2 (over core).
Axes of the slice: x: 2, y: 2, z: 4, core: 2. Of those that a mesh axis runs over, the one named last changes fastest.
Arguments:
- features: bfloat16 [32, 8, 16384], P(None, None, ('gx', 'gy')), may hold values from 0.09 to 3.1
- cost_weights: float32 [32], replicated, may hold values from 0.1 to 1
- successors: int32 [8, 16384], P(None, ('gx', 'gy')), may hold values from 0 to 1535, as said below
- turn_valid: int32 [8, 16384], P(None, ('gx', 'gy')), may hold values from 0 to 1, as said below
- border_lists: int32 [4, 2048], P(None, ('gx', 'gy')), may hold values from 0 to 1023, as said below
- destinations: int32 [32], P('dst'), may hold values from 0 to 16383
- anchors: float32 [32, 16384], P('dst', ('gx', 'gy')), may hold values from 0.25 to 4
- demo_counts: int32 [8, 16384], P(None, ('gx', 'gy')), may hold values from 0 to 3
Outputs:
- count_gap: float32 [8, 16384], P(None, ('gx', 'gy'))
- gradient: float32 [32], replicated
Inputs may be any that keep to these rules, and one draw needn't show every extreme that they name: `successors`: values below 1024 are segments of the same block and turn 0 is always one of them; 1024 + k * 128 + j is entry j of the border list of the neighbour on side k (0: one gx position lower, 1: higher, 2: one gy position lower, 3: higher) that faces this block. `turn_valid`: turn 0 is always 1; a turn into a side where the grid has no neighbouring block is 0. `border_lists`: within one block and side the 128 entries are distinct local segment numbers.
All inputs are finite; a program needn't handle non-finite values.
Results may differ from a plain program's by a relative error of at most 0.0003.
Values sent between devices are 32-bit elements; how exact they have to be, the bound alone decides.
No kernel may reach another device: no remote copies, remote signals or barrier semaphores. Data moves between devices by JAX's collectives and lax.ppermute only.
A program may use at most 64 MiB of HBM per device.

v0:
```python
import functools

import jax
import jax.numpy as jnp
from jax import lax
from jax.experimental import pallas as pl
from jax.experimental.pallas import tpu as pltpu
from jax.sharding import PartitionSpec as P

HORIZON = 8
NEG = -1e30
START_COST = 100.0
LANES = 128
ROWS = 60
RANKS = -(-ROWS // 16) * 16
STEP = 14
USUAL = 56
DEPTH = -(-ROWS // STEP) * STEP
BLOCK_AXES = ("gy", "gx")

LANE_PICK = lax.GatherDimensionNumbers(
    offset_dims=(),
    collapsed_slice_dims=(1,),
    start_index_map=(1,),
    operand_batching_dims=(0,),
    start_indices_batching_dims=(0,),
)


def lane_gather(table, index):
    return lax.gather(
        table,
        index[..., None],
        LANE_PICK,
        (1, 1),
        mode=lax.GatherScatterMode.PROMISE_IN_BOUNDS,
    )


def tree_select(picked, bits):
    level = list(picked)
    for bit in bits:
        if len(level) == 1:
            break
        nxt = []
        for n in range(0, len(level), 2):
            if n + 1 < len(level):
                nxt.append(jnp.where(bit, level[n + 1], level[n]))
            else:
                nxt.append(level[n])
        level = nxt
    return level[0]


def row_bits(index, count):
    return [(index & (LANES << i)) != 0 for i in range(count)]


def table_gather(table_rows, index):
    lane = index & (LANES - 1)
    bits = row_bits(index, max(len(table_rows) - 1, 1).bit_length())
    return tree_select([lane_gather(row, lane) for row in table_rows], bits)


def run_copies(copies):
    for copy in copies:
        copy.start()
    for copy in copies:
        copy.wait()


def of_blocks(ref, half, row, per_block):
    return ref[pl.ds(half * 8 * per_block + row, 8, stride=per_block), :]


def whole_copies(pairs, sem):
    return [pltpu.make_async_copy(src, dst, sem.at[n]) for n, (src, dst) in enumerate(pairs)]


def by_core(what, mine, other):
    first = lax.axis_index("dst") == 0
    pl.when(first)(lambda: what(mine, other))
    pl.when(jnp.logical_not(first))(lambda: what(other, mine))


def own_block(grid_x):
    return lax.axis_index("gy") * grid_x + lax.axis_index("gx")


def renumbered(segment, per_block, blocks, grid_x):
    grid_y = blocks // grid_x
    block, place = lax.div(segment, per_block), lax.rem(segment, per_block)
    return (lax.rem(block, grid_y) * grid_x + lax.div(block, grid_y)) * per_block + place


def padded_rows(rows):
    tiles = -(-rows // 8)
    return (tiles + 1 - tiles % 2) * 8


def target_mask(dest, half, chunk, per_block):
    sub = lax.broadcasted_iota(jnp.int32, (8, LANES), 0)
    lane = lax.broadcasted_iota(jnp.int32, (8, LANES), 1)
    return (half * 8 + sub) * per_block + chunk * LANES + lane == dest


def arrange_kernel(
    succ_any, valid_any, border_any, anchor_any, reward_ref, out_any,
    succ_ref, valid_ref, border_ref, anchor_ref, split_ref, out_ref, count_ref, first_ref, order_ref, inverse_ref, placed_ref,
    pair_ref, lane_ref, code_ref, column_ref, acc_ref, sem
):
    run_copies(
        whole_copies(
            [
                (succ_any, succ_ref),
                (valid_any, valid_ref),
                (border_any, border_ref),
                (anchor_any, anchor_ref),
            ],
            sem,
        )
    )
    turns, width = succ_ref.shape
    chunks = width // LANES
    slots = chunks + 4
    step = 2 * LANES
    tops = 16
    square = (LANES, LANES)
    down = lax.broadcasted_iota(jnp.int32, square, 0)
    along = lax.broadcasted_iota(jnp.int32, square, 1)
    down_f, along_f = down.astype(jnp.float32), along.astype(jnp.float32)
    before = down < along
    unit = jnp.where(down == along, 1.0, 0.0)
    lane_row = lax.broadcasted_iota(jnp.int32, (LANES, step), 0)
    top_row = lax.broadcasted_iota(jnp.int32, (tops, step), 0)
    rank_row = lax.broadcasted_iota(jnp.int32, (RANKS, step), 0).astype(jnp.float32)
    last_dims = (((1,), (1,)), ((), ()))

    def product(left, right):
        return lax.dot_general(left, right, last_dims, preferred_element_type=jnp.float32)

    def columns(rows):
        return lax.dot_general(
            unit, rows, last_dims, precision=lax.Precision.HIGHEST, preferred_element_type=jnp.float32
        )

    def summed_down(array):
        return jnp.sum(array, axis=0, keepdims=True)

    def place_of(row, col):
        return summed_down(jnp.where((col > row) | ((col == row) & before), 1.0, 0.0))

    def count(a, total):
        for c in range(width // step):
            cols = slice(c * step, (c + 1) * step)
            u = succ_ref[pl.ds(a, 1), cols]
            low = jnp.where(valid_ref[pl.ds(a, 1), cols] == 1, u & (LANES - 1), -1)
            hot_low = jnp.where(low == lane_row, 1.0, 0.0).astype(jnp.bfloat16)
            hot_top = jnp.where((u >> 7) == top_row, 1.0, 0.0).astype(jnp.bfloat16)
            total = total + product(hot_top, hot_low)
        return total

    counts = lax.fori_loop(0, turns, count, jnp.zeros((tops, LANES), jnp.float32), unroll=2)
    count_columns = columns(counts)
    out_ref[...] = jnp.zeros_like(out_ref)
    for ref in (count_ref, first_ref, order_ref, inverse_ref, placed_ref, pair_ref):
        ref[...] = jnp.zeros_like(ref)
    for n in range(slots):
        i = n if n < chunks else n - chunks
        place = place_of(counts[n : n + 1, :], count_columns[:, n : n + 1])
        place = place if i % 2 == 0 else (LANES - 1.0) - place
        if (i // 2) % 2:
            place = jnp.where(place >= LANES // 2, place - LANES // 2, place + LANES // 2)
        first_ref[n : n + 1, :] = place
    first_columns = columns(first_ref[...])
    for n in range(slots):
        hit = first_columns[:, n : n + 1] == along_f
        inverse_ref[n : n + 1, :] = summed_down(jnp.where(hit, down_f, 0.0))
        placed_ref[n : n + 1, :] = summed_down(jnp.where(hit, count_columns[:, n : n + 1], 0.0))
    local = summed_down(placed_ref[0:chunks, :])
    room = -summed_down(placed_ref[chunks:tops, :])
    pair_ref[0:1, :] = local
    pair_ref[1:2, :] = room
    pair = columns(pair_ref[...])
    local_place, room_place = place_of(local, pair[:, 0:1]), place_of(room, pair[:, 1:2])
    pair_ref[0:1, :] = local_place
    pair_ref[1:2, :] = room_place
    pair = columns(pair_ref[...])
    goes = summed_down(jnp.where(pair[:, 1:2] == local_place, down_f, 0.0))
    comes = summed_down(jnp.where(pair[:, 0:1] == room_place, down_f, 0.0))
    full = (chunks, LANES)
    comes = jnp.broadcast_to(comes, full).astype(jnp.int32)
    goes = jnp.broadcast_to(goes, full)
    order_ref[0:chunks, :] = lane_gather(goes, first_ref[0:chunks, :].astype(jnp.int32))
    order_ref[chunks:tops, :] = first_ref[chunks:tops, :]
    inverse_ref[0:chunks, :] = lane_gather(inverse_ref[0:chunks, :], comes)
    placed_ref[0:chunks, :] = lane_gather(placed_ref[0:chunks, :], comes)
    running = jnp.zeros((1, LANES), jnp.float32)
    for n in range(slots):
        count_ref[n : n + 1, :] = running
        running = running + placed_ref[n : n + 1, :]
        out_ref[ROWS + n : ROWS + n + 1, :] = running
        out_ref[ROWS + slots + n : ROWS + slots + n + 1, :] = order_ref[n : n + 1, :]
        out_ref[ROWS + 2 * slots + n : ROWS + 2 * slots + n + 1, :] = inverse_ref[n : n + 1, :]
    for k in range(chunks):
        cols = slice(k * LANES, (k + 1) * LANES)
        u = succ_ref[:, cols]
        rows = [jnp.broadcast_to(order_ref[n : n + 1, :], (turns, LANES)) for n in range(slots)]
        lane = jnp.where(valid_ref[:, cols] == 1, table_gather(rows, u), -1.0)
        code = jnp.where(lane >= 0.0, lane + ((u >> 7) * LANES).astype(jnp.float32), -1.0)
        lane_ref[:, cols] = lane
        code_ref[:, cols] = code
        column_ref[cols, :] = columns(code)
    acc_ref[...] = jnp.zeros_like(acc_ref)
    earlier = jnp.where(
        lax.broadcasted_iota(jnp.int32, (step, step), 0) < lax.broadcasted_iota(jnp.int32, (step, step), 1),
        1.0,
        0.0,
    )
    lane_row_f = lane_row.astype(jnp.float32)

    def one_chunk(c, base):
        start = pl.multiple_of(c * step, step)
        cols = pl.ds(start, step)
        s = start + lax.broadcasted_iota(jnp.int32, (1, step), 1)
        source = [
            (s & ~7).astype(jnp.float32).astype(jnp.bfloat16),
            (s & 7).astype(jnp.float32).astype(jnp.bfloat16),
        ]
        for a in range(turns):
            row = slice(a, a + 1)
            hot = jnp.where(lane_ref[row, cols] == lane_row_f, 1.0, 0.0).astype(jnp.bfloat16)
            hot_top = jnp.where((succ_ref[row, cols] >> 7) == top_row, 1.0, 0.0)
            same = column_ref[cols, row] == code_ref[row, cols]
            within = summed_down(jnp.where(same, earlier, 0.0))
            coarse = (base.astype(jnp.int32) & ~127).astype(jnp.float32)
            both = jnp.concatenate([coarse, base - coarse], axis=0).astype(jnp.bfloat16)
            starts = jnp.dot(both, hot, preferred_element_type=jnp.float32)
            begin = summed_down((starts[:tops] + starts[tops:]) * hot_top)
            base = base + product(hot_top.astype(jnp.bfloat16), hot)
            match = jnp.where(begin + within == rank_row, 1.0, 0.0).astype(jnp.bfloat16)
            r = reward_ref[row, cols]
            r1 = r.astype(jnp.bfloat16)
            rest = r - r1.astype(jnp.float32)
            r2 = rest.astype(jnp.bfloat16)
            r3 = (rest - r2.astype(jnp.float32)).astype(jnp.bfloat16)
            left = jnp.concatenate([match * piece for piece in (*source, r1, r2, r3)], axis=0)
            acc_ref[...] += product(left, hot)
        return base

    lax.fori_loop(0, width // step, one_chunk, count_ref[...])
    part = [acc_ref[i * RANKS : i * RANKS + ROWS, :] for i in range(5)]
    share = out_ref.shape[0] // 2
    out_ref[0:ROWS, :] = part[0] + part[1]
    out_ref[share : share + ROWS, :] = (part[2] + part[3]) + part[4]
    listed = columns(border_ref[...].astype(jnp.float32)).astype(jnp.int32)
    for side in range(4):
        for q in range(chunks):
            found = jnp.where(listed[:, side : side + 1] == along + q * LANES, down_f + 1.0, 0.0)
            row = share + ROWS + side * chunks + q
            out_ref[row : row + 1, :] = summed_down(found)
    blocks = anchor_ref.shape[0]
    for q in range(chunks):
        split_ref[pl.ds(q, blocks, chunks), :] = anchor_ref[:, q * LANES : (q + 1) * LANES]
    half = out_ref.at[pl.ds(pl.multiple_of(lax.axis_index("dst") * share, 8), share)]
    size = share + chunks
    pairs = []
    for b in range(blocks):
        pairs.append((half, out_any.at[pl.ds(b * size, share)]))
        pairs.append((split_ref.at[pl.ds(b * chunks, chunks)], out_any.at[pl.ds(b * size + share, chunks)]))
    run_copies(whole_copies(pairs, sem))


def graph_kernel(
    weight_ref, feature_any, succ_any, valid_any, border_any, out_ref, reward_ref,
    feature_ref, succ_ref, valid_ref, border_ref, part_ref, sem
):
    run_copies(
        whole_copies(
            [
                (feature_any, feature_ref),
                (succ_any, succ_ref),
                (valid_any, valid_ref),
                (border_any, border_ref),
            ],
            sem,
        )
    )
    turns, width = succ_ref.shape
    chunks = width // LANES
    edges = turns * chunks
    part_ref[edges : edges + 8, :] = jnp.zeros((8, LANES), jnp.float32)
    part_ref[edges : edges + 4, :] = border_ref[...].astype(jnp.float32)
    first_core = lax.axis_index("dst") == 0
    for q in range(chunks):
        cols = slice(q * LANES, (q + 1) * LANES)
        cost = weight_ref[0] * feature_ref[0, :, cols].astype(jnp.float32)
        for f in range(1, feature_ref.shape[0]):
            cost = cost + weight_ref[f] * feature_ref[f, :, cols].astype(jnp.float32)
        reward_ref[:, cols] = -cost
        masked = jnp.where(valid_ref[:, cols] == 1, -cost, NEG)
        turn_to = succ_ref[:, cols].astype(jnp.float32)
        part_ref[pl.ds(q, turns, chunks), :] = jnp.where(first_core, masked, turn_to)
    common = part_ref.shape[0]
    for b in range(out_ref.shape[0] // common):
        out_ref[b * common : (b + 1) * common, :] = part_ref[...]


def regroup_kernel(pieces_ref, out_ref):
    halves, rows = out_ref.shape[:2]
    size = pieces_ref.shape[0] // (8 * halves)
    for h in range(halves):

        def one_row(i, carry, h=h):
            out_ref[h, i] = of_blocks(pieces_ref, h, i, size)
            return carry

        lax.fori_loop(0, rows, one_row, 0, unroll=8)


def weigh(out):
    top = functools.reduce(jnp.maximum, out)
    raised = [jnp.exp(score - top) for score in out]
    return top, raised, functools.reduce(jnp.add, raised)


def weighed_turns(values, reward, index, h, q, turns, chunks):
    tables = [values[h, r] for r in range(chunks + 4)]
    out = []
    for a in range(turns):
        rows = tables if a else tables[:chunks]
        out.append(reward[h, a * chunks + q] + table_gather(rows, index[h, a * chunks + q]))
    return weigh(out)


def policy_kernel(values_ref, reward_ref, index_ref, raised_ref, max_ref, inv_ref):
    halves, chunks = max_ref.shape[:2]
    turns = reward_ref.shape[1] // chunks

    def one_chunk(q, inner):
        for h in range(halves):
            top, raised, total = weighed_turns(values_ref, reward_ref, index_ref, h, q, turns, chunks)
            max_ref[h, q] = top
            inv_ref[h, q] = 1.0 / total
            for a in range(turns):
                raised_ref[h, a * chunks + q] = raised[a]
        return inner

    lax.fori_loop(0, chunks, one_chunk, 0, unroll=chunks)


def value_kernel(
    grid_x, dest_ref, mine_ref, other_ref, ext_ref, reward, index, border, side_pad, spare_ref
):
    halves = ext_ref.shape[0]
    blocks = 8 * halves
    chunks = ext_ref.shape[1] - 4
    edges = reward.shape[1]
    turns = edges // chunks
    per_block = chunks * LANES
    dest = renumbered(dest_ref[own_block(grid_x)], per_block, blocks, grid_x)
    side_pad[...] = jnp.zeros_like(side_pad)
    sub = lax.broadcasted_iota(jnp.int32, (8, LANES), 0)
    lane = lax.broadcasted_iota(jnp.int32, (8, LANES), 1)
    dest_block, dest_place = lax.div(dest, per_block), lax.rem(dest, per_block)

    def unpack(first, second):
        for h in range(halves):

            def rows(i, carry, h=h):
                reward[h, i] = first[h, i]
                index[h, i] = second[h, i].astype(jnp.int32)
                return carry

            lax.fori_loop(0, edges, rows, 0, unroll=8)
            for side in range(4):
                border[h, side] = first[h, edges + side].astype(jnp.int32)

    by_core(unpack, mine_ref, other_ref)
    for h in range(halves):
        for side in range(4):
            found = (border[h, side] == dest_place) & (h * 8 + sub == dest_block)
            entry = jnp.max(jnp.where(found, lane + 1, 0).astype(jnp.float32), axis=1, keepdims=True)
            side_pad[side, 8 + 8 * h : 16 + 8 * h, :] = jnp.broadcast_to(entry, (8, LANES))
    shifts = ((1, -1), (0, 1), (3, -grid_x), (2, grid_x))

    def shown(h, side):
        facing, by = shifts[side]
        start = 8 + 8 * h + by
        return side_pad[facing, start : start + 8, :]

    def dest_index(h):
        where = jnp.where(h * 8 + sub == dest_block, dest_place, -1)
        for side in range(4):
            entry = shown(h, side).astype(jnp.int32)
            where = jnp.where(entry > 0, per_block + side * LANES + entry - 1, where)
        return where

    def bring_halo(values):
        for h in range(halves):
            table = [values[h, q] for q in range(chunks)]
            for side in range(4):
                side_pad[side, 8 + 8 * h : 16 + 8 * h, :] = table_gather(table, border[h, side])
        for h in range(halves):
            for side in range(4):
                values[h, chunks + side] = shown(h, side)

    def store_value(h, q, top, total, into):
        value = top + jnp.log(total)
        into[h, q] = jnp.where(target_mask(dest, h, q, per_block), 0.0, value)

    wanted = [dest_index(h) for h in range(halves)]

    def first_chunk(q, inner):
        for h in range(halves):
            out = []
            for a in range(turns):
                before = jnp.where(index[h, a * chunks + q] == wanted[h], 0.0, -START_COST)
                out.append(reward[h, a * chunks + q] + before)
            top, _, total = weigh(out)
            store_value(h, q, top, total, spare_ref)
        return inner

    lax.fori_loop(0, chunks, first_chunk, 0, unroll=2)

    def backup(values, into):
        bring_halo(values)

        def one_chunk(q, inner):
            for h in range(halves):
                top, _, total = weighed_turns(values, reward, index, h, q, turns, chunks)
                store_value(h, q, top, total, into)
            return inner

        lax.fori_loop(0, chunks, one_chunk, 0, unroll=chunks)

    def two_backups(step, carry):
        backup(spare_ref, ext_ref)
        backup(ext_ref, spare_ref)
        return carry

    lax.fori_loop(0, (HORIZON - 2) // 2, two_backups, 0)
    backup(spare_ref, ext_ref)
    bring_halo(ext_ref)


def push_kernel(
    grid_x, scale, dest_ref, mine_ref, other_ref, graph_mine, graph_other, ext_ref, raised_ref, max_ref,
    inv_ref, keep_ref, send_ref, counts, ends, order, values, source, slot, going, policy, flows, back, scaled, total, arrived, side_pad, raw
):
    halves = ext_ref.shape[0]
    blocks = 8 * halves
    share = mine_ref.shape[1]
    chunks = max_ref.shape[1]
    edges = raised_ref.shape[1]
    turns = edges // chunks
    per_block = chunks * LANES
    slots = chunks + 4
    dest = renumbered(dest_ref[own_block(grid_x)], per_block, blocks, grid_x)
    core = lax.axis_index("dst")
    side_pad[...] = jnp.zeros_like(side_pad)

    def unpack(first, second):
        for h in range(halves):
            for n in range(slots):
                ends[h, n] = first[h, ROWS + n]
                order[h, n] = first[h, ROWS + slots + n].astype(jnp.int32)
                inverse = first[h, ROWS + 2 * slots + n].astype(jnp.int32)
                values[h, n] = lane_gather(ext_ref[h, n], inverse)

            def rows(r, carry, h=h):
                source[h, r] = first[h, r].astype(jnp.int32)
                policy[h, r] = second[h, r]
                return carry

            lax.fori_loop(0, ROWS, rows, 0, unroll=6)
            for r in range(ROWS, DEPTH):
                source[h, r] = jnp.zeros((8, LANES), jnp.int32)
                policy[h, r] = jnp.zeros((8, LANES), jnp.float32)
            for n in range(4 * chunks):
                back[h, n] = second[h, ROWS + n].astype(jnp.int32) - 1

    by_core(unpack, mine_ref, other_ref)
    deepest = jnp.max(functools.reduce(jnp.maximum, [ends[h, slots - 1] for h in range(halves)]))
    deepest = deepest.astype(jnp.int32)
    fits = deepest <= ROWS
    steps = jnp.where(deepest <= USUAL, USUAL // STEP, DEPTH // STEP)
    shifts = ((1, -1), (0, 1), (3, -grid_x), (2, grid_x))

    def shown(h, side):
        facing, by = shifts[side]
        start = 8 + 8 * h + by
        return side_pad[facing, start : start + 8, :]

    @pl.when(jnp.logical_not(fits))
    def _():
        for h in range(halves):
            for n in range(slots):
                order[h, n] = lax.broadcasted_iota(jnp.int32, (8, LANES), 1)

    for h in range(halves):
        for side in range(4):
            side_pad[side, 8 + 8 * h : 16 + 8 * h, :] = order[h, chunks + side].astype(jnp.float32)
    for h in range(halves):
        for side in range(4):
            lanes = shown(h, side).astype(jnp.int32)
            for q in range(chunks):
                entry = back[h, side * chunks + q]
                back[h, side * chunks + q] = jnp.where(
                    entry >= 0, lane_gather(lanes, jnp.maximum(entry, 0)), -1
                )

    def prepare_rows(rows):
        row_before = [None] * halves
        for i, r in enumerate(rows):
            for h in range(halves):
                src = source[h, r]
                place = jnp.asarray(r).astype(jnp.float32)
                row = functools.reduce(
                    jnp.add, [jnp.where(ends[h, n] <= place, 1, 0) for n in range(slots)]
                )
                slot[h, r] = row
                if i:
                    going[h, r] = jnp.where(row == row_before[h], 1.0, 0.0)
                row_before[h] = row
                bits = [(row & (1 << n)) != 0 for n in range(4)]
                picked = tree_select([values[h, n] for n in range(slots)], bits)
                top = table_gather([max_ref[h, q] for q in range(chunks)], src)
                policy[h, r] = jnp.exp(policy[h, r] + picked - top)

    def prepare_step(t, carry):
        prepare_rows([t * STEP + i for i in range(STEP)])
        return carry

    usual = deepest <= USUAL
    pl.when(usual)(lambda: prepare_rows(range(USUAL)))
    lax.fori_loop(0, jnp.where(usual, 0, steps), prepare_step, 0)
    for h in range(halves):
        for q in range(chunks):
            own = mine_ref[h, share - chunks + q]
            first = jnp.where(target_mask(dest, h, q, per_block), 0.0, own)
            total[h, q] = first
            scaled[h, q] = first * inv_ref[h, q]

    @pl.when(jnp.logical_not(fits))
    def _():
        def keep_turns(first, second):
            for h in range(halves):

                def rows(e, carry, h=h):
                    raw[h, e] = second[h, e].astype(jnp.int32)
                    return carry

                lax.fori_loop(0, edges, rows, 0)

        by_core(keep_turns, graph_mine, graph_other)

    zero = jnp.zeros((8, LANES), jnp.float32)

    def keep(h):
        for side in range(4):
            side_pad[side, 8 + 8 * h : 16 + 8 * h, :] = arrived[h, chunks + side]

    def add_flow(acc, row, flow):
        return [acc[n] + jnp.where(row == n, flow, 0.0) for n in range(slots)]

    def sum_arranged():
        for h in range(halves):
            for n in range(slots):
                arrived[h, n] = zero

        def one_step(t, carry):
            tables = [[scaled[h, q] for q in range(chunks)] for h in range(halves)]
            step_sums = [[zero] * slots for h in range(halves)]
            so_far = [None] * halves
            for i in range(STEP):
                r = t * STEP + i
                for h in range(halves):
                    flow = table_gather(tables[h], source[h, r]) * policy[h, r]
                    so_far[h] = flow + going[h, r] * so_far[h] if i else flow
                    row = slot[h, r]
                    step_sums[h] = [jnp.where(row == n, so_far[h], step_sums[h][n]) for n in range(slots)]
            for h in range(halves):
                for n in range(slots):
                    arrived[h, n] = arrived[h, n] + step_sums[h][n]
            return carry

        def usual_rows():
            for h in range(halves):
                table = [scaled[h, q] for q in range(chunks)]
                for r in range(USUAL):
                    flow = table_gather(table, source[h, r]) * policy[h, r]
                    so_far = flow + going[h, r] * so_far if r else flow
                    flows[h, r] = so_far
            for h in range(halves):
                sums = [zero] * slots
                for r in range(USUAL):
                    row, so_far = slot[h, r], flows[h, r]
                    sums = [jnp.where(row == n, so_far, sums[n]) for n in range(slots)]
                for n in range(slots):
                    arrived[h, n] = sums[n]

        pl.when(usual)(usual_rows)
        lax.fori_loop(0, jnp.where(usual, 0, steps), one_step, 0)
        for h in range(halves):
            keep(h)

    def sum_turned():
        lane = lax.broadcasted_iota(jnp.int32, (8, LANES), 1)
        for h in range(halves):

            def one_edge_row(e, acc, h=h):
                flow = scaled[h, lax.rem(e, chunks)] * raised_ref[h, e]
                where = raw[h, e]

                def one_turn(k, state):
                    flow, where, acc = state[0], state[1], list(state[2:])
                    here = jnp.where((where & (LANES - 1)) == lane, where >> 7, -1)
                    acc = add_flow(acc, here, flow)
                    return (pltpu.roll(flow, 1, 1), pltpu.roll(where, 1, 1), *acc)

                return tuple(lax.fori_loop(0, LANES, one_turn, (flow, where, *acc))[2:])

            for n, value in enumerate(lax.fori_loop(0, edges, one_edge_row, (zero,) * slots)):
                arrived[h, n] = value
            keep(h)

    def push(round_index, carry):
        pl.when(fits)(sum_arranged)
        pl.when(jnp.logical_not(fits))(sum_turned)
        for h in range(halves):
            landed = [shown(h, side) for side in range(4)]
            for q in range(chunks):
                value = lane_gather(arrived[h, q], order[h, q])
                for side in range(4):
                    entry = back[h, side * chunks + q]
                    got = lane_gather(landed[side], jnp.maximum(entry, 0))
                    value = value + jnp.where(entry >= 0, got, 0.0)
                value = jnp.where(target_mask(dest, h, q, per_block), 0.0, value)
                total[h, q] = total[h, q] + value
                scaled[h, q] = value * inv_ref[h, q]
        return carry

    lax.fori_loop(0, HORIZON - 1, push, 0)
    rows_out = edges // 2
    apart = counts.shape[1] // blocks
    for h in range(halves):
        for q in range(chunks):
            weight = total[h, q] * inv_ref[h, q] * scale
            for part, piece in ((core, 0), (1 - core, 1)):
                for a in range(turns // 2):
                    value = weight * raised_ref[h, (part * (turns // 2) + a) * chunks + q]
                    start = h * 8 * apart + a * chunks + q
                    counts[piece, pl.ds(start, 8, stride=apart), :] = value
    for piece, out_ref in ((0, keep_ref), (1, send_ref)):
        for b in range(blocks):
            out_ref[b * rows_out : (b + 1) * rows_out, :] = counts[
                piece, b * apart : b * apart + rows_out, :
            ]


VMEM_SPEC = pl.BlockSpec(memory_space=pltpu.VMEM)
SMEM_SPEC = pl.BlockSpec(memory_space=pltpu.SMEM)
HBM_SPEC = pl.BlockSpec(memory_space=pltpu.HBM)
PARAMS = pltpu.CompilerParams(vmem_limit_bytes=48 * 1024 * 1024)


def f32(*shape):
    return jax.ShapeDtypeStruct(shape, jnp.float32)


def call_graph(cost_weights, features, successors, turn_valid, border_lists, blocks):
    turns, width = successors.shape
    chunks = width // LANES
    rows = turns * chunks + 8
    return pl.pallas_call(
        graph_kernel,
        out_shape=(f32(blocks * rows, LANES), f32(turns, width)),
        in_specs=[SMEM_SPEC] + [HBM_SPEC] * 4,
        out_specs=(VMEM_SPEC, VMEM_SPEC),
        scratch_shapes=[
            pltpu.VMEM(features.shape, features.dtype),
            pltpu.VMEM(successors.shape, jnp.int32),
            pltpu.VMEM(turn_valid.shape, jnp.int32),
            pltpu.VMEM(border_lists.shape, jnp.int32),
            pltpu.VMEM((rows, LANES), jnp.float32),
            pltpu.SemaphoreType.DMA((4,)),
        ],
        compiler_params=pltpu.CompilerParams(vmem_limit_bytes=63 * 1024 * 1024),
        name="own_graph",
    )(cost_weights, features, successors, turn_valid, border_lists)


def arranged_rows(chunks):
    most = ROWS + max(3 * (chunks + 4), 4 * chunks)
    return -(-most // 8) * 8


def call_arrange(successors, turn_valid, border_lists, anchors, reward):
    chunks = successors.shape[1] // LANES
    share = arranged_rows(chunks)
    blocks = anchors.shape[0]
    return pl.pallas_call(
        arrange_kernel,
        out_shape=f32(blocks * (share + chunks), LANES),
        in_specs=[HBM_SPEC] * 4 + [VMEM_SPEC],
        out_specs=HBM_SPEC,
        scratch_shapes=[
            pltpu.VMEM(successors.shape, jnp.int32),
            pltpu.VMEM(turn_valid.shape, jnp.int32),
            pltpu.VMEM(border_lists.shape, jnp.int32),
            pltpu.VMEM(anchors.shape, jnp.float32),
            pltpu.VMEM((blocks * chunks, LANES), jnp.float32),
            pltpu.VMEM((2 * share, LANES), jnp.float32),
            *[pltpu.VMEM((16, LANES), jnp.float32)] * 5,
            pltpu.VMEM((8, LANES), jnp.float32),
            pltpu.VMEM(successors.shape, jnp.float32),
            pltpu.VMEM(successors.shape, jnp.float32),
            pltpu.VMEM(successors.shape[::-1], jnp.float32),
            pltpu.VMEM((5 * RANKS, LANES), jnp.float32),
            pltpu.SemaphoreType.DMA((2 * blocks,)),
        ],
        compiler_params=PARAMS,
        cost_estimate=pl.CostEstimate(flops=4_000_000_000, bytes_accessed=400_000, transcendentals=0),
        name="arrange_turns",
    )(successors, turn_valid, border_lists, anchors, reward)


def call_regroup(pieces, blocks):
    return pl.pallas_call(
        regroup_kernel,
        out_shape=f32(blocks // 8, pieces.shape[0] // blocks, 8, LANES),
        in_specs=[VMEM_SPEC],
        out_specs=VMEM_SPEC,
        compiler_params=PARAMS,
        name="regroup",
    )(pieces)


def call_values(destinations, mine, other, blocks, grid_x, turns, chunks):
    halves = blocks // 8
    edges = turns * chunks
    rows = (halves, edges, 8, LANES)
    return pl.pallas_call(
        functools.partial(value_kernel, grid_x),
        out_shape=(
            f32(halves, chunks + 4, 8, LANES),
            f32(*rows),
            jax.ShapeDtypeStruct(rows, jnp.int32),
        ),
        in_specs=[SMEM_SPEC, VMEM_SPEC, VMEM_SPEC],
        out_specs=(VMEM_SPEC,) * 3,
        scratch_shapes=[
            pltpu.VMEM((halves, 4, 8, LANES), jnp.int32),
            pltpu.VMEM((4, blocks + 16, LANES), jnp.float32),
            pltpu.VMEM((halves, chunks + 4, 8, LANES), jnp.float32),
        ],
        compiler_params=PARAMS,
        cost_estimate=pl.CostEstimate(flops=40_000_000, bytes_accessed=40_000_000, transcendentals=2_000_000),
        name="soft_values",
    )(destinations, mine, other)


def call_policy(ext, reward, index):
    halves, edges = reward.shape[:2]
    chunks = ext.shape[1] - 4
    return pl.pallas_call(
        policy_kernel,
        out_shape=(f32(*reward.shape), f32(halves, chunks, 8, LANES), f32(halves, chunks, 8, LANES)),
        in_specs=[VMEM_SPEC] * 3,
        out_specs=(VMEM_SPEC,) * 3,
        compiler_params=PARAMS,
        cost_estimate=pl.CostEstimate(flops=5_000_000, bytes_accessed=5_000_000, transcendentals=200_000),
        name="policy",
    )(ext, reward, index)


def call_push(destinations, mine, other, graph_mine, graph_other, ext, raised, top, inv, grid_x, scale):
    halves, edges = raised.shape[:2]
    blocks = 8 * halves
    chunks = top.shape[1]

    def vmem(rows, dtype=jnp.float32):
        return pltpu.VMEM((halves, rows, 8, LANES), dtype)

    return pl.pallas_call(
        functools.partial(push_kernel, grid_x, scale),
        out_shape=(f32(blocks * edges // 2, LANES),) * 2,
        in_specs=[SMEM_SPEC] + [VMEM_SPEC] * 8,
        out_specs=(VMEM_SPEC,) * 2,
        scratch_shapes=[
            pltpu.VMEM((2, blocks * padded_rows(edges // 2), LANES), jnp.float32),
            vmem(chunks + 4),
            vmem(chunks + 4, jnp.int32),
            vmem(chunks + 4),
            vmem(DEPTH, jnp.int32),
            vmem(DEPTH, jnp.int32),
            vmem(DEPTH),
            vmem(DEPTH),
            vmem(USUAL),
            vmem(4 * chunks, jnp.int32),
            vmem(chunks),
            vmem(chunks),
            vmem(chunks + 4),
            pltpu.VMEM((4, blocks + 16, LANES), jnp.float32),
            vmem(edges, jnp.int32),
        ],
        compiler_params=PARAMS,
        name="push_mass",
    )(destinations, mine, other, graph_mine, graph_other, ext, raised, top, inv)


def to_blocks(array):
    return lax.all_to_all(array, BLOCK_AXES, 0, 0, tiled=True)


def other_core(array):
    return lax.ppermute(array, "dst", [(0, 1), (1, 0)])


def per_destination(
    features, cost_weights, successors, turn_valid, border_lists, destinations, anchors, demo_counts
):
    turns, own_count = successors.shape
    chunks = own_count // LANES
    edges = turns * chunks
    grid_x = lax.axis_size("gx")
    blocks = lax.axis_size("gy") * grid_x
    groups = lax.axis_size("dst")
    pieces, reward = call_graph(cost_weights, features, successors, turn_valid, border_lists, blocks)
    graph = to_blocks(pieces)
    arranged = call_arrange(successors, turn_valid, border_lists, anchors, reward)
    core = lax.axis_index("dst")
    demo_term = jnp.where(turn_valid == 1, demo_counts, 0).astype(jnp.float32) / 3.0
    own_feats = lax.dynamic_slice_in_dim(features, core * (turns // 2), turns // 2, axis=1)
    first_core, own_feats, demo_term, arranged = lax.optimization_barrier(
        (core == 0, own_feats, demo_term, arranged)
    )
    graph = call_regroup(lax.optimization_barrier((graph, arranged))[0], blocks)
    graph, arranged = lax.optimization_barrier((graph, arranged))
    graph = (graph, other_core(graph))
    arranged = to_blocks(arranged)
    ext, reward, index = call_values(destinations, *graph, blocks, grid_x, turns, chunks)
    arranged, ext = lax.optimization_barrier((arranged, ext))
    arranged = call_regroup(arranged, blocks)
    arranged, ext = lax.optimization_barrier((arranged, ext))
    arranged = (arranged, other_core(arranged))
    values = (ext, *call_policy(ext, reward, index))
    scale = 1.0 / (anchors.shape[0] * groups * HORIZON)
    kept, sent = call_push(destinations, *arranged, *graph, *values, grid_x, scale)
    halved = (kept + other_core(sent)).reshape(blocks, edges // 2, LANES)
    half = jnp.sum(to_blocks(halved), axis=0)
    other = other_core(half)
    part = (turns // 2, own_count)
    own_gap = lax.dynamic_slice_in_dim(demo_term, core * part[0], part[0]) - half.reshape(part)
    own_feats = own_feats.astype(jnp.float32)
    block_term = jnp.sum(own_gap[None] * own_feats, axis=(1, 2)) / (own_count * blocks)
    visits = jnp.concatenate([jnp.where(first_core, half, other), jnp.where(first_core, other, half)])
    count_gap = demo_term - visits.reshape(turns, own_count)
    terms = jnp.broadcast_to(block_term, (groups * blocks, 1, block_term.shape[0]))
    terms = lax.all_to_all(terms, (*BLOCK_AXES, "dst"), 0, 0, tiled=True)
    terms, count_gap = lax.optimization_barrier((terms, count_gap))
    return count_gap, jnp.sum(terms, axis=(0, 1))


def passed_along(array, axis, by):
    length = lax.axis_size(axis)
    pairs = [(i, i + by) for i in range(length) if 0 <= i + by < length]
    return lax.ppermute(array, axis, pairs)


def bring_values(values, border_lists):
    outgoing = values[:, border_lists]
    north_part = passed_along(outgoing[:, 1], "gx", 1)
    south_part = passed_along(outgoing[:, 0], "gx", -1)
    west_part = passed_along(outgoing[:, 3], "gy", 1)
    east_part = passed_along(outgoing[:, 2], "gy", -1)
    return jnp.concatenate([north_part, south_part, west_part, east_part], axis=1)


def return_flow(arrived, border_lists, own_count, border_width):
    local_part = arrived[:, :own_count]
    halo_part = arrived[:, own_count:].reshape(arrived.shape[0], 4, border_width)
    from_south = passed_along(halo_part[:, 0], "gx", -1)
    from_north = passed_along(halo_part[:, 1], "gx", 1)
    from_east = passed_along(halo_part[:, 2], "gy", -1)
    from_west = passed_along(halo_part[:, 3], "gy", 1)
    returned = jnp.stack([from_north, from_south, from_west, from_east], axis=1)
    return local_part.at[:, border_lists].add(returned)


def select_cells(cells, flat_index, turn_shape):
    picked = jnp.take(cells, flat_index, axis=1)
    return picked.reshape(cells.shape[0], turn_shape[0], turn_shape[1])


def turn_scores(values, halo_cells, reward, flat_turns, usable):
    extended = jnp.concatenate([values, halo_cells], axis=1)
    scores = reward[None] + select_cells(extended, flat_turns, usable.shape)
    return jnp.where(usable[None], scores, NEG)


def per_block(
    features, cost_weights, successors, turn_valid, border_lists, destinations, anchors, demo_counts
):
    own_count = successors.shape[1]
    border_width = border_lists.shape[1]
    dest_count = anchors.shape[0]
    slot_total = own_count + 4 * border_width
    block_index = lax.axis_index("gx") * lax.axis_size("gy") + lax.axis_index("gy")
    positions = jnp.arange(own_count, dtype=jnp.int32)
    is_target = positions[None, :] == (destinations - block_index * own_count)[:, None]
    usable = turn_valid == 1
    feats = features.astype(jnp.float32)
    reward = -jnp.sum(feats * cost_weights[:, None, None], axis=0)
    flat_turns = successors.reshape(-1)
    values = jnp.where(is_target, 0.0, -START_COST).astype(jnp.float32)
    for round_index in range(HORIZON):
        halo_cells = bring_values(values, border_lists)
        scores = turn_scores(values, halo_cells, reward, flat_turns, usable)
        row_max = jnp.max(scores, axis=1)
        new_values = row_max + jnp.log(jnp.sum(jnp.exp(scores - row_max[:, None]), axis=1))
        values = jnp.where(is_target, 0.0, new_values)
    halo_cells = bring_values(values, border_lists)
    scores = turn_scores(values, halo_cells, reward, flat_turns, usable)
    row_max = jnp.max(scores, axis=1)
    raised = jnp.exp(scores - row_max[:, None])
    policy = raised / jnp.sum(raised, axis=1, keepdims=True)
    mass_now = jnp.where(is_target, 0.0, anchors)
    turn_counts = jnp.zeros(successors.shape, jnp.float32)
    for round_index in range(HORIZON):
        turn_flow = mass_now[:, None, :] * policy
        turn_counts = turn_counts + jnp.sum(turn_flow, axis=0)
        if round_index + 1 < HORIZON:
            arrived = (
                jnp.zeros((dest_count, slot_total), jnp.float32)
                .at[:, flat_turns]
                .add(turn_flow.reshape(dest_count, -1))
            )
            landed = return_flow(arrived, border_lists, own_count, border_width)
            mass_now = jnp.where(is_target, 0.0, landed)
    local_visits = turn_counts / (dest_count * lax.axis_size("dst") * HORIZON)
    visits = lax.psum(local_visits, "dst")
    demo_term = jnp.where(usable, demo_counts, 0).astype(jnp.float32) / 3.0
    count_gap = demo_term - visits
    total_segments = own_count * lax.axis_size("gx") * lax.axis_size("gy")
    own_gap = demo_term / lax.axis_size("dst") - local_visits
    block_term = jnp.sum(own_gap[None] * feats, axis=(1, 2)) / total_segments
    gradient = lax.psum(block_term, ("gx", "gy", "dst"))
    return (count_gap, gradient)


def local(features, cost_weights, successors, turn_valid, border_lists, destinations, anchors, demo_counts):
    args = (
        features, cost_weights, successors, turn_valid, border_lists, destinations, anchors, demo_counts
    )
    blocks = lax.axis_size("gx") * lax.axis_size("gy")
    fits = (
        anchors.shape[0] == blocks
        and blocks % 8 == 0
        and lax.axis_size("dst") == 2
        and lax.axis_size("gx") in (2, 4, 8)
        and lax.axis_size("gy") in (2, 4, 8)
        and successors.shape[1] == 8 * LANES
        and border_lists.shape[1] == LANES
    )
    return per_destination(*args) if fits else per_block(*args)


def solution(mesh):
    in_specs = (
        P(None, None, ("gx", "gy")),
        P(),
        P(None, ("gx", "gy")),
        P(None, ("gx", "gy")),
        P(None, ("gx", "gy")),
        P("dst"),
        P("dst", ("gx", "gy")),
        P(None, ("gx", "gy")),
    )
    out_specs = (P(None, ("gx", "gy")), P())
    return jax.shard_map(local, mesh=mesh, in_specs=in_specs, out_specs=out_specs, check_vma=False)
```

profile of v0, /device:TPU:0, one launch (start us, length us, event | category | flops | bytes accessed | tf_op | source)
XLA Modules:
  0.0 98.7 jit_solution(1097727979405364982)
XLA Ops:
  0.6 2.7 %own_graph.1 = (f32[1152,128]{1,0:T(8,128)}, f32[8,1024]{1,0:T(8,128)}) custom-call(f32[32]{0:T(128)} %weight_ref.1, bf16[32,8,1024]{2,1,0:T(8,128)(2,1)} %feature_any.1, s32[8,1024]{1,0:T(8,128)} %succ_any.3, s32[8,1024]{1,0:T(8,128)} %valid_any.3, s32[4,128]{1,0:T(4,128)} %border_any.3), custom_call_target="tpu_custom_call" | custom-call | tf_op jit(solution)/shard_map/own_graph/pallas_call | solution.py:676
  3.4 0.0 copy-start.6
  3.4 8.5 %all-to-all-start = ((f32[16,72,128]{2,1,0:T(8,128)}), f32[16,72,128]{2,1,0:T(8,128)S(1)}, u32[]{:S(2)}, u32[]{:S(2)}) async-start(f32[16,72,128]{2,1,0:T(8,128)} %bitcast.8), calls=%async_computation | async-start | bytes 1179648 | tf_op jit(solution)/shard_map/all_to_all | solution.py:814
  11.9 0.1 constant_dynamic-slice_fusion
  12.1 0.6 copy-done
  12.6 0.0 copy-done.7
  12.7 0.1 copy-done.4
  12.8 0.7 copy-done.1
  13.4 0.0 copy-done.5
  13.5 11.7 %arrange_turns.1 = f32[1664,128]{1,0:T(8,128)} custom-call(s32[8,1024]{1,0:T(8,128)S(1)} %copy-done.1, s32[8,1024]{1,0:T(8,128)S(1)} %copy-done, s32[4,128]{1,0:T(4,128)S(1)} %copy-done.2, f32[16,1024]{1,0:T(8,128)S(1)} %copy-done.4, f32[8,1024]{1,0:T(8,128)S(1)} %copy-done.5), custom_call_target="tpu_custom_call" | custom-call | flops 4000000000 | bytes 400000 | tf_op jit(solution)/shard_map/arrange_turns/pallas_call | solution.py:703
  25.1 3.0 %all-to-all-done = f32[16,72,128]{2,1,0:T(8,128)S(1)} async-done(((f32[16,72,128]{2,1,0:T(8,128)}), f32[16,72,128]{2,1,0:T(8,128)S(1)}, u32[]{:S(2)}, u32[]{:S(2)}) %all-to-all-start) | async-done | bytes 589856 | tf_op jit(solution)/shard_map/all_to_all | solution.py:814
  28.1 0.1 regroup.2.mine_ref.graph_mine
  28.3 4.2 %all-to-all-start.1 = ((f32[16,104,128]{2,1,0:T(8,128)}), f32[16,104,128]{2,1,0:T(8,128)S(1)}, u32[]{:S(2)}, u32[]{:S(2)}) async-start(f32[16,104,128]{2,1,0:T(8,128)} %bitcast.2), calls=%async_computation.1 | async-start | bytes 1703936 | tf_op jit(solution)/shard_map/all_to_all | solution.py:814
  32.5 0.1 collective-permute-start
  32.6 2.0 %collective-permute-done.other_ref.graph_other = f32[2,72,8,128]{3,2,1,0:T(8,128)S(1)} collective-permute-done((f32[2,72,8,128]{3,2,1,0:T(8,128)S(1)}, f32[2,72,8,128]{3,2,1,0:T(8,128)S(1)}, u32[]{:S(2)}, u32[]{:S(2)}) %collective-permute-start) | collective-permute-done | bytes 589856 | tf_op jit(solution)/shard_map/ppermute | solution.py:818
  34.6 16.4 %soft_values.1 = (f32[2,12,8,128]{3,2,1,0:T(8,128)S(1)}, f32[2,64,8,128]{3,2,1,0:T(8,128)S(1)}, s32[2,64,8,128]{3,2,1,0:T(8,128)S(1)}) custom-call(s32[16]{0:T(128)S(1)} %copy-done.3, f32[2,72,8,128]{3,2,1,0:T(8,128)S(1)} %regroup.2.mine_ref.graph_mine, f32[2,72,8,128]{3,2,1,0:T(8,128)S(1)} %collective-permute-done.other_ref.graph_other), custom_call_target="tpu_custom_call" | custom-call | flops 40000000 | bytes 40000000 | tf_op jit(solution)/shard_map/soft_values/pallas_call | solution.py:744
  51.0 1.6 %all-to-all-done.1 = f32[16,104,128]{2,1,0:T(8,128)S(1)} async-done(((f32[16,104,128]{2,1,0:T(8,128)}), f32[16,104,128]{2,1,0:T(8,128)S(1)}, u32[]{:S(2)}, u32[]{:S(2)}) %all-to-all-start.1) | async-done | bytes 852000 | tf_op jit(solution)/shard_map/all_to_all | solution.py:814
  52.6 0.2 regroup.3.mine_ref
  52.8 0.1 collective-permute-start.1
  52.9 2.1 %policy.1 = (f32[2,64,8,128]{3,2,1,0:T(8,128)S(1)}, f32[2,8,8,128]{3,2,1,0:T(8,128)S(1)}, f32[2,8,8,128]{3,2,1,0:T(8,128)S(1)}) custom-call(f32[2,12,8,128]{3,2,1,0:T(8,128)S(1)} %get-tuple-element.36.values_ref.ext_ref, f32[2,64,8,128]{3,2,1,0:T(8,128)S(1)} %get-tuple-element.37.reward_ref, s32[2,64,8,128]{3,2,1,0:T(8,128)S(1)} %get-tuple-element.38.index_ref), custom_call_target="tpu_custom_call" | custom-call | flops 5000000 | bytes 5000000 | tf_op jit(solution)/shard_map/policy/pallas_call | solution.py:767
  55.0 0.3 collective-permute-done.1.other_ref
  55.2 15.1 %push_mass.1 = (f32[512,128]{1,0:T(8,128)S(1)}, f32[512,128]{1,0:T(8,128)S(1)}) custom-call(s32[16]{0:T(128)S(1)} %copy-done.3, f32[2,104,8,128]{3,2,1,0:T(8,128)S(1)} %regroup.3.mine_ref, f32[2,104,8,128]{3,2,1,0:T(8,128)S(1)} %collective-permute-done.1.other_ref, f32[2,72,8,128]{3,2,1,0:T(8,128)S(1)} %regroup.2.mine_ref.graph_mine, ...), custom_call_target="tpu_custom_call" | custom-call | tf_op jit(solution)/shard_map/push_mass/pallas_call | solution.py:786
  70.3 0.3 collective-permute-start.2
  70.6 1.3 %collective-permute-done.2 = f32[512,128]{1,0:T(8,128)S(1)} collective-permute-done((f32[512,128]{1,0:T(8,128)S(1)}, f32[512,128]{1,0:T(8,128)S(1)}, u32[]{:S(2)}, u32[]{:S(2)}) %collective-permute-start.2) | collective-permute-done | bytes 262176 | tf_op jit(solution)/shard_map/ppermute | solution.py:818
  71.9 15.4 %all_to_all.34 = f32[16,32,128]{2,1,0:T(8,128)S(1)} all-to-all(f32[16,32,128]{2,1,0:T(8,128)S(1)} %bitcast.7), channel_id=1, replica_groups=mesh['gx'=4,'gy'=4,'dst'=2] {'gy','gx'}, dimensions={0} | all-to-all | bytes 524288 | tf_op jit(solution)/shard_map/all_to_all | solution.py:814
  87.3 0.1 collective-permute-start.3
  87.4 0.3 multiply_reduce_fusion
  87.8 0.6 broadcast_in_dim.9
  88.4 2.6 %all-to-all-start.3 = ((f32[32,1,32]{2,1,0:T(1,128)}), f32[32,1,32]{2,1,0:T(1,128)S(1)}, u32[]{:S(2)}, u32[]{:S(2)}) async-start(f32[32,1,32]{2,1,0:T(1,128)} %broadcast_in_dim.9), calls=%async_computation.3 | async-start | bytes 32768 | tf_op jit(solution)/shard_map/all_to_all | solution.py:861
  91.1 0.6 sub.7
  91.7 6.5 %all-to-all-done.3 = f32[32,1,32]{2,1,0:T(1,128)S(1)} async-done(((f32[32,1,32]{2,1,0:T(1,128)}), f32[32,1,32]{2,1,0:T(1,128)S(1)}, u32[]{:S(2)}, u32[]{:S(2)}) %all-to-all-start.3) | async-done | bytes 4128 | tf_op jit(solution)/shard_map/all_to_all | solution.py:861
  98.2 0.6 reduce_sum.29
  (20 shorter events, 0.1 us)
Async XLA Ops:
  3.4 8.5 %copy-start.6 = (bf16[32,8,1024]{2,1,0:T(8,128)(2,1)S(1)}, bf16[32,8,1024]{2,1,0:T(8,128)(2,1)}, u32[]{:S(2)}) copy-start(bf16[32,8,1024]{2,1,0:T(8,128)(2,1)} %feature_any.1) | copy-start | bytes 1572868
  3.4 24.7 %all-to-all-start = ((f32[16,72,128]{2,1,0:T(8,128)}), f32[16,72,128]{2,1,0:T(8,128)S(1)}, u32[]{:S(2)}, u32[]{:S(2)}) async-start(f32[16,72,128]{2,1,0:T(8,128)} %bitcast.8), calls=%async_computation | async-start | bytes 1179648 | tf_op jit(solution)/shard_map/all_to_all | solution.py:814
  11.9 0.8 copy-start
  11.9 0.8 copy-start.7
  11.9 0.9 copy-start.4
  12.7 0.8 copy-start.1
  12.7 0.8 copy-start.2
  12.7 0.8 copy-start.5
  28.3 6.3 %copy-start.3 = (s32[16]{0:T(128)S(1)}, s32[16]{0:T(128)}, u32[]{:S(2)}) copy-start(s32[16]{0:T(128)} %dest_ref.3) | copy-start | bytes 196
  28.3 24.3 %all-to-all-start.1 = ((f32[16,104,128]{2,1,0:T(8,128)}), f32[16,104,128]{2,1,0:T(8,128)S(1)}, u32[]{:S(2)}, u32[]{:S(2)}) async-start(f32[16,104,128]{2,1,0:T(8,128)} %bitcast.2), calls=%async_computation.1 | async-start | bytes 1703936 | tf_op jit(solution)/shard_map/all_to_all | solution.py:814
  32.5 2.1 %collective-permute-start = (f32[2,72,8,128]{3,2,1,0:T(8,128)S(1)}, f32[2,72,8,128]{3,2,1,0:T(8,128)S(1)}, u32[]{:S(2)}, u32[]{:S(2)}) collective-permute-start(f32[2,72,8,128]{3,2,1,0:T(8,128)S(1)} %regroup.2.mine_ref.graph_mine), channel_id=1, source_target_pairs={{0,1},{1,0},{2,3},{3,2},{4,5},{5,4},{6,7},{7,6},{8,9},{9,8},{10,11... | collective-permute-start | bytes 1769480 | tf_op jit(solution)/shard_map/ppermute | solution.py:818
  52.8 2.4 %collective-permute-start.1 = (f32[2,104,8,128]{3,2,1,0:T(8,128)S(1)}, f32[2,104,8,128]{3,2,1,0:T(8,128)S(1)}, u32[]{:S(2)}, u32[]{:S(2)}) collective-permute-start(f32[2,104,8,128]{3,2,1,0:T(8,128)S(1)} %regroup.3.mine_ref), channel_id=1, source_target_pairs={{0,1},{1,0},{2,3},{3,2},{4,5},{5,4},{6,7},{7,6},{8,9},{9,8},{10,11... | collective-permute-start | bytes 2555912 | tf_op jit(solution)/shard_map/ppermute | solution.py:818
  70.3 1.6 %collective-permute-start.2 = (f32[512,128]{1,0:T(8,128)S(1)}, f32[512,128]{1,0:T(8,128)S(1)}, u32[]{:S(2)}, u32[]{:S(2)}) collective-permute-start(f32[512,128]{1,0:T(8,128)S(1)} %get-tuple-element.43), channel_id=1, source_target_pairs={{0,1},{1,0},{2,3},{3,2},{4,5},{5,4},{6,7},{7,6},{8,9},{9,8},{10,11... | collective-permute-start | bytes 786440 | tf_op jit(solution)/shard_map/ppermute | solution.py:818
  87.3 3.7 %collective-permute-start.3 = (f32[32,128]{1,0:T(8,128)S(1)}, f32[32,128]{1,0:T(8,128)S(1)}, u32[]{:S(2)}, u32[]{:S(2)}) collective-permute-start(f32[32,128]{1,0:T(8,128)S(1)} %reduce_sum.27), channel_id=1, source_target_pairs={{0,1},{1,0},{2,3},{3,2},{4,5},{5,4},{6,7},{7,6},{8,9},{9,8},{10,11... | collective-permute-start | bytes 49160 | tf_op jit(solution)/shard_map/ppermute | solution.py:818
  88.4 9.8 %all-to-all-start.3 = ((f32[32,1,32]{2,1,0:T(1,128)}), f32[32,1,32]{2,1,0:T(1,128)S(1)}, u32[]{:S(2)}, u32[]{:S(2)}) async-start(f32[32,1,32]{2,1,0:T(1,128)} %broadcast_in_dim.9), calls=%async_computation.3 | async-start | bytes 32768 | tf_op jit(solution)/shard_map/all_to_all | solution.py:861
where the time goes:
time: 99.2 us; the launch traced here: 98.7 us
  Pallas kernels  48.3 us (49%)
  starting transfers between devices  15.8 us (16%)
  blocking collectives  15.4 us (16%)
  waiting for transfers between devices  14.6 us (15%)
  local copies, waits for them, and re-layouts  2.18 us (2%)
  other arithmetic  1.6 us (2%)
    pallas_call x1, Pallas kernels, call_values(): pl.pallas_call(functools.partial(value_kernel, grid_x), out_shape=(f32(ha...  16.4 us
    all_to_all x1, blocking collectives, to_blocks(): return lax.all_to_all(array, BLOCK_AXES, 0, 0, tiled=True)  15.4 us
    pallas_call x1, Pallas kernels, call_push(): pl.pallas_call(functools.partial(push_kernel, grid_x, scale), out_shape=(...  15.1 us
    all_to_all x2, starting transfers between devices, to_blocks(): return lax.all_to_all(array, BLOCK_AXES, 0, 0, tiled=True)  12.6 us
    pallas_call x1, Pallas kernels, call_arrange(): pl.pallas_call(arrange_kernel, out_shape=f32(blocks * (share + chunks), L...  11.7 us
    all_to_all x1, waiting for transfers between devices, per_destination(): terms = lax.all_to_all(terms, (*BLOCK_AXES, 'dst'), 0, 0, tiled=True)  6.47 us
    all_to_all x2, waiting for transfers between devices, to_blocks(): return lax.all_to_all(array, BLOCK_AXES, 0, 0, tiled=True)  4.59 us
    ppermute x4, waiting for transfers between devices, other_core(): return lax.ppermute(array, 'dst', [(0, 1), (1, 0)])  3.57 us
  transfers between devices with their start and end apart: 7, of which 6 were waited for; matrix products, arithmetic and copies ran while one was open for 2% of the time, Pallas kernels for 31%

commit v1 on v0

--- a/solution.py
+++ b/solution.py
@@ -201,7 +201,8 @@
         running = running + placed_ref[n : n + 1, :]
         out_ref[ROWS + n : ROWS + n + 1, :] = running
         out_ref[ROWS + slots + n : ROWS + slots + n + 1, :] = order_ref[n : n + 1, :]
-        out_ref[ROWS + 2 * slots + n : ROWS + 2 * slots + n + 1, :] = inverse_ref[n : n + 1, :]
+        row = inverse_row(n, slots)
+        out_ref[row : row + 1, :] = inverse_ref[n : n + 1, :]
     for k in range(chunks):
         cols = slice(k * LANES, (k + 1) * LANES)
         u = succ_ref[:, cols]
@@ -262,18 +263,31 @@
     blocks = anchor_ref.shape[0]
     for q in range(chunks):
         split_ref[pl.ds(q, blocks, chunks), :] = anchor_ref[:, q * LANES : (q + 1) * LANES]
-    half = out_ref.at[pl.ds(pl.multiple_of(lax.axis_index("dst") * share, 8), share)]
-    size = share + chunks
+    start = pl.multiple_of(lax.axis_index("dst") * share, 8)
+    common = share - chunks
+    shared = out_ref[pl.ds(start + common, chunks), :]
+    sub = lax.broadcasted_iota(jnp.int32, (chunks, LANES), 0)
+    own_rows = (lax.axis_index("dst") == 0) & (sub >= 4)
+    for b in range(blocks):
+        rows = slice(b * chunks, (b + 1) * chunks)
+        split_ref[rows, :] = jnp.where(own_rows, split_ref[rows, :], shared)
+    half = out_ref.at[pl.ds(start, common)]
     pairs = []
     for b in range(blocks):
-        pairs.append((half, out_any.at[pl.ds(b * size, share)]))
-        pairs.append((split_ref.at[pl.ds(b * chunks, chunks)], out_any.at[pl.ds(b * size + share, chunks)]))
+        pairs.append((half, out_any.at[pl.ds(b * share, common)]))
+        pairs.append((split_ref.at[pl.ds(b * chunks, chunks)], out_any.at[pl.ds(b * share + common, chunks)]))
     run_copies(whole_copies(pairs, sem))
 
 
+def inverse_row(n, slots):
+    if n < slots - 4:
+        return ROWS + 2 * slots + n
+    return 2 * (ROWS + 3 * slots) - slots + n
+
+
 def graph_kernel(
-    weight_ref, feature_any, succ_any, valid_any, border_any, out_ref, reward_ref,
-    feature_ref, succ_ref, valid_ref, border_ref, part_ref, sem
+    weight_ref, feature_any, succ_any, valid_any, border_any, anchor_any, out_ref, reward_ref,
+    feature_ref, succ_ref, valid_ref, border_ref, anchor_ref, part_ref, split_ref, sem
 ):
     run_copies(
         whole_copies(
@@ -282,6 +296,7 @@
                 (succ_any, succ_ref),
                 (valid_any, valid_ref),
                 (border_any, border_ref),
+                (anchor_any, anchor_ref),
             ],
             sem,
         )
@@ -291,6 +306,8 @@
     edges = turns * chunks
     part_ref[edges : edges + 8, :] = jnp.zeros((8, LANES), jnp.float32)
     part_ref[edges : edges + 4, :] = border_ref[...].astype(jnp.float32)
+    blocks = anchor_ref.shape[0]
+    split_ref[0:8, :] = jnp.zeros((8, LANES), jnp.float32)
     first_core = lax.axis_index("dst") == 0
     for q in range(chunks):
         cols = slice(q * LANES, (q + 1) * LANES)
@@ -301,9 +318,16 @@
         masked = jnp.where(valid_ref[:, cols] == 1, -cost, NEG)
         turn_to = succ_ref[:, cols].astype(jnp.float32)
         part_ref[pl.ds(q, turns, chunks), :] = jnp.where(first_core, masked, turn_to)
-    common = part_ref.shape[0]
-    for b in range(out_ref.shape[0] // common):
-        out_ref[b * common : (b + 1) * common, :] = part_ref[...]
+        split_ref[pl.ds(8 + q, blocks, chunks), :] = anchor_ref[:, cols]
+    size = part_ref.shape[0]
+    lists = part_ref[edges:size, :]
+    upper = lax.broadcasted_iota(jnp.int32, (8, LANES), 0) < 4
+    for b in range(blocks):
+        out_ref[b * size : b * size + edges, :] = part_ref[0:edges, :]
+        own = split_ref[8 + b * chunks : 16 + b * chunks, :]
+        lower = split_ref[4 + b * chunks : 12 + b * chunks, :]
+        mixed = jnp.where(upper, lists, lower)
+        out_ref[b * size + edges : (b + 1) * size, :] = jnp.where(first_core, mixed, own)
 
 
 def regroup_kernel(pieces_ref, out_ref):
@@ -465,7 +489,8 @@
             for n in range(slots):
                 ends[h, n] = first[h, ROWS + n]
                 order[h, n] = first[h, ROWS + slots + n].astype(jnp.int32)
-                inverse = first[h, ROWS + 2 * slots + n].astype(jnp.int32)
+                row = inverse_row(n, slots)
+                inverse = (first[h, row] if row < share else second[h, row - share]).astype(jnp.int32)
                 values[h, n] = lane_gather(ext_ref[h, n], inverse)
 
             def rows(r, carry, h=h):
@@ -481,6 +506,20 @@
                 back[h, n] = second[h, ROWS + n].astype(jnp.int32) - 1
 
     by_core(unpack, mine_ref, other_ref)
+
+    def first_anchors():
+        for h in range(halves):
+            for q in range(4):
+                total[h, q] = graph_mine[h, edges + 4 + q]
+                total[h, 4 + q] = mine_ref[h, share - 4 + q]
+
+    def second_anchors():
+        for h in range(halves):
+            for q in range(chunks):
+                total[h, q] = graph_mine[h, edges + q]
+
+    pl.when(core == 0)(first_anchors)
+    pl.when(core != 0)(second_anchors)
     deepest = jnp.max(functools.reduce(jnp.maximum, [ends[h, slots - 1] for h in range(halves)]))
     deepest = deepest.astype(jnp.int32)
     fits = deepest <= ROWS
@@ -537,8 +576,7 @@
     lax.fori_loop(0, jnp.where(usual, 0, steps), prepare_step, 0)
     for h in range(halves):
         for q in range(chunks):
-            own = mine_ref[h, share - chunks + q]
-            first = jnp.where(target_mask(dest, h, q, per_block), 0.0, own)
+            first = jnp.where(target_mask(dest, h, q, per_block), 0.0, total[h, q])
             total[h, q] = first
             scaled[h, q] = first * inv_ref[h, q]
 
@@ -586,19 +624,20 @@
             return carry
 
         def usual_rows():
-            for h in range(halves):
-                table = [scaled[h, q] for q in range(chunks)]
+            for h in range(halves + 1):
+                sums = [zero] * slots
+                table = [scaled[h, q] for q in range(chunks)] if h < halves else None
                 for r in range(USUAL):
-                    flow = table_gather(table, source[h, r]) * policy[h, r]
-                    so_far = flow + going[h, r] * so_far if r else flow
-                    flows[h, r] = so_far
-            for h in range(halves):
-                sums = [zero] * slots
-                for r in range(USUAL):
-                    row, so_far = slot[h, r], flows[h, r]
-                    sums = [jnp.where(row == n, so_far, sums[n]) for n in range(slots)]
-                for n in range(slots):
-                    arrived[h, n] = sums[n]
+                    if h < halves:
+                        flow = table_gather(table, source[h, r]) * policy[h, r]
+                        so_far = flow + going[h, r] * so_far if r else flow
+                        flows[h, r] = so_far
+                    if h:
+                        row, summed = slot[h - 1, r], flows[h - 1, r]
+                        sums = [jnp.where(row == n, summed, sums[n]) for n in range(slots)]
+                if h:
+                    for n in range(slots):
+                        arrived[h - 1, n] = sums[n]
 
         pl.when(usual)(usual_rows)
         lax.fori_loop(0, jnp.where(usual, 0, steps), one_step, 0)
@@ -669,40 +708,38 @@
     return jax.ShapeDtypeStruct(shape, jnp.float32)
 
 
-def call_graph(cost_weights, features, successors, turn_valid, border_lists, blocks):
+def call_graph(cost_weights, features, successors, turn_valid, border_lists, anchors):
     turns, width = successors.shape
+    blocks = anchors.shape[0]
     chunks = width // LANES
     rows = turns * chunks + 8
     return pl.pallas_call(
         graph_kernel,
         out_shape=(f32(blocks * rows, LANES), f32(turns, width)),
-        in_specs=[SMEM_SPEC] + [HBM_SPEC] * 4,
+        in_specs=[SMEM_SPEC] + [HBM_SPEC] * 5,
         out_specs=(VMEM_SPEC, VMEM_SPEC),
         scratch_shapes=[
             pltpu.VMEM(features.shape, features.dtype),
             pltpu.VMEM(successors.shape, jnp.int32),
             pltpu.VMEM(turn_valid.shape, jnp.int32),
             pltpu.VMEM(border_lists.shape, jnp.int32),
+            pltpu.VMEM(anchors.shape, jnp.float32),
             pltpu.VMEM((rows, LANES), jnp.float32),
-            pltpu.SemaphoreType.DMA((4,)),
+            pltpu.VMEM((blocks * chunks + 8, LANES), jnp.float32),
+            pltpu.SemaphoreType.DMA((5,)),
         ],
         compiler_params=pltpu.CompilerParams(vmem_limit_bytes=63 * 1024 * 1024),
         name="own_graph",
-    )(cost_weights, features, successors, turn_valid, border_lists)
-
-
-def arranged_rows(chunks):
-    most = ROWS + max(3 * (chunks + 4), 4 * chunks)
-    return -(-most // 8) * 8
+    )(cost_weights, features, successors, turn_valid, border_lists, anchors)
 
 
 def call_arrange(successors, turn_valid, border_lists, anchors, reward):
     chunks = successors.shape[1] // LANES
-    share = arranged_rows(chunks)
+    share = ROWS + 3 * (chunks + 4)
     blocks = anchors.shape[0]
     return pl.pallas_call(
         arrange_kernel,
-        out_shape=f32(blocks * (share + chunks), LANES),
+        out_shape=f32(blocks * share, LANES),
         in_specs=[HBM_SPEC] * 4 + [VMEM_SPEC],
         out_specs=HBM_SPEC,
         scratch_shapes=[
@@ -827,7 +864,7 @@
     grid_x = lax.axis_size("gx")
     blocks = lax.axis_size("gy") * grid_x
     groups = lax.axis_size("dst")
-    pieces, reward = call_graph(cost_weights, features, successors, turn_valid, border_lists, blocks)
+    pieces, reward = call_graph(cost_weights, features, successors, turn_valid, border_lists, anchors)
     graph = to_blocks(pieces)
     arranged = call_arrange(successors, turn_valid, border_lists, anchors, reward)
     core = lax.axis_index("dst")
@@ -836,10 +873,10 @@
     first_core, own_feats, demo_term, arranged = lax.optimization_barrier(
         (core == 0, own_feats, demo_term, arranged)
     )
-    graph = call_regroup(lax.optimization_barrier((graph, arranged))[0], blocks)
-    graph, arranged = lax.optimization_barrier((graph, arranged))
+    graph = lax.optimization_barrier((graph, arranged))[0]
+    arranged = to_blocks(arranged)
+    graph = call_regroup(graph, blocks)
     graph = (graph, other_core(graph))
-    arranged = to_blocks(arranged)
     ext, reward, index = call_values(destinations, *graph, blocks, grid_x, turns, chunks)
     arranged, ext = lax.optimization_barrier((arranged, ext))
     arranged = call_regroup(arranged, blocks)
@@ -963,6 +1000,7 @@
         and lax.axis_size("gy") in (2, 4, 8)
         and successors.shape[1] == 8 * LANES
         and border_lists.shape[1] == LANES
+        and successors.shape[0] == 8
     )
     return per_destination(*args) if fits else per_block(*args)
 

time: 99.2 us -> 99.8 us (level)
  waiting for transfers between devices: 14.6 us -> 13.1 us
  blocking collectives: 15.4 us -> 16.8 us
    all_to_all x1, blocking collectives: 15.4 us -> 16.8 us  [to_blocks(): return lax.all_to_all(array, BLOCK_AXES, 0, 0, tiled=True)]
    all_to_all x2, waiting for transfers between devices: 4.59 us -> 3.29 us  [to_blocks(): return lax.all_to_all(array, BLOCK_AXES, 0, 0, tiled=True)]
where the time goes in v1:
time: 99.8 us; the launch traced here: 99.2 us
  Pallas kernels  48.8 us (49%)
  blocking collectives  16.8 us (17%)
  starting transfers between devices  15.8 us (16%)
  waiting for transfers between devices  13.1 us (13%)
  local copies, waits for them, and re-layouts  2.21 us (2%)
  other arithmetic  1.6 us (2%)
    all_to_all x1, blocking collectives, to_blocks(): return lax.all_to_all(array, BLOCK_AXES, 0, 0, tiled=True)  16.8 us
    pallas_call x1, Pallas kernels, call_values(): pl.pallas_call(functools.partial(value_kernel, grid_x), out_shape=(f32(ha...  16.4 us
    pallas_call x1, Pallas kernels, call_push(): pl.pallas_call(functools.partial(push_kernel, grid_x, scale), out_shape=(...  15.2 us
    all_to_all x2, starting transfers between devices, to_blocks(): return lax.all_to_all(array, BLOCK_AXES, 0, 0, tiled=True)  12.6 us
    pallas_call x1, Pallas kernels, call_arrange(): pl.pallas_call(arrange_kernel, out_shape=f32(blocks * share, LANES), in_s...  11.7 us
    all_to_all x1, waiting for transfers between devices, per_destination(): terms = lax.all_to_all(terms, (*BLOCK_AXES, 'dst'), 0, 0, tiled=True)  6.47 us
    ppermute x4, waiting for transfers between devices, other_core(): return lax.ppermute(array, 'dst', [(0, 1), (1, 0)])  3.38 us
    all_to_all x2, waiting for transfers between devices, to_blocks(): return lax.all_to_all(array, BLOCK_AXES, 0, 0, tiled=True)  3.29 us
  transfers between devices with their start and end apart: 7, of which 6 were waited for; matrix products, arithmetic and copies ran while one was open for 2% of the time, Pallas kernels for 31%

profile of v1, /device:TPU:0, one launch (start us, length us, event | category | flops | bytes accessed | tf_op | source)
XLA Modules:
  0.0 99.2 jit_solution(15734338716478266196)
XLA Ops:
  0.6 2.8 %own_graph.1 = (f32[1152,128]{1,0:T(8,128)}, f32[8,1024]{1,0:T(8,128)}) custom-call(f32[32]{0:T(128)} %weight_ref.1, bf16[32,8,1024]{2,1,0:T(8,128)(2,1)} %feature_any.1, s32[8,1024]{1,0:T(8,128)} %succ_any.3, s32[8,1024]{1,0:T(8,128)} %valid_any.3, s32[4,128]{1,0:T(4,128)} %border_any.3, f32[16,1024]{1,0:T(8,128)} %anchor_any.3), custom_call_target="tpu_custom_call" | custom-call | tf_op jit(solution)/shard_map/own_graph/pallas_call | solution.py:716
  3.4 0.0 copy-start.6
  3.4 8.5 %all-to-all-start.1 = ((f32[16,72,128]{2,1,0:T(8,128)}), f32[16,72,128]{2,1,0:T(8,128)S(1)}, u32[]{:S(2)}, u32[]{:S(2)}) async-start(f32[16,72,128]{2,1,0:T(8,128)} %bitcast.8), calls=%async_computation.1 | async-start | bytes 1179648 | tf_op jit(solution)/shard_map/all_to_all | solution.py:851
  11.9 0.0 copy-start.3
  11.9 0.1 constant_dynamic-slice_fusion
  12.1 0.6 copy-done
  12.7 0.0 copy-done.7
  12.7 0.0 copy-done.5
  12.7 0.8 copy-done.1
  13.5 11.7 %arrange_turns.1 = f32[1536,128]{1,0:T(8,128)} custom-call(s32[8,1024]{1,0:T(8,128)S(1)} %copy-done.2, s32[8,1024]{1,0:T(8,128)S(1)} %copy-done, s32[4,128]{1,0:T(4,128)S(1)} %copy-done.3, f32[16,1024]{1,0:T(8,128)S(1)} %copy-done.1, f32[8,1024]{1,0:T(8,128)S(1)} %copy-done.5), custom_call_target="tpu_custom_call" | custom-call | flops 4000000000 | bytes 400000 | tf_op jit(solution)/shard_map/arrange_turns/pallas_call | solution.py:740
  25.2 3.0 %all-to-all-done.1 = f32[16,72,128]{2,1,0:T(8,128)S(1)} async-done(((f32[16,72,128]{2,1,0:T(8,128)}), f32[16,72,128]{2,1,0:T(8,128)S(1)}, u32[]{:S(2)}, u32[]{:S(2)}) %all-to-all-start.1) | async-done | bytes 589856 | tf_op jit(solution)/shard_map/all_to_all | solution.py:851
  28.2 4.2 %all-to-all-start = ((f32[16,96,128]{2,1,0:T(8,128)}), f32[16,96,128]{2,1,0:T(8,128)S(1)}, u32[]{:S(2)}, u32[]{:S(2)}) async-start(f32[16,96,128]{2,1,0:T(8,128)} %bitcast), calls=%async_computation | async-start | bytes 1572864 | tf_op jit(solution)/shard_map/all_to_all | solution.py:851
  32.3 0.2 regroup.2.mine_ref.graph_mine
  32.5 0.1 collective-permute-start
  32.6 2.0 %collective-permute-done.other_ref.graph_other = f32[2,72,8,128]{3,2,1,0:T(8,128)S(1)} collective-permute-done((f32[2,72,8,128]{3,2,1,0:T(8,128)S(1)}, f32[2,72,8,128]{3,2,1,0:T(8,128)S(1)}, u32[]{:S(2)}, u32[]{:S(2)}) %collective-permute-start) | collective-permute-done | bytes 589856 | tf_op jit(solution)/shard_map/ppermute | solution.py:855
  34.6 16.4 %soft_values.1 = (f32[2,12,8,128]{3,2,1,0:T(8,128)S(1)}, f32[2,64,8,128]{3,2,1,0:T(8,128)S(1)}, s32[2,64,8,128]{3,2,1,0:T(8,128)S(1)}) custom-call(s32[16]{0:T(128)S(1)} %copy-done.4, f32[2,72,8,128]{3,2,1,0:T(8,128)S(1)} %regroup.2.mine_ref.graph_mine, f32[2,72,8,128]{3,2,1,0:T(8,128)S(1)} %collective-permute-done.other_ref.graph_other), custom_call_target="tpu_custom_call" | custom-call | flops 40000000 | bytes 40000000 | tf_op jit(solution)/shard_map/soft_values/pallas_call | solution.py:781
  51.0 0.3 all-to-all-done
  51.3 0.6 regroup.3.mine_ref
  51.9 0.1 collective-permute-start.1
  52.0 2.1 %policy.1 = (f32[2,64,8,128]{3,2,1,0:T(8,128)S(1)}, f32[2,8,8,128]{3,2,1,0:T(8,128)S(1)}, f32[2,8,8,128]{3,2,1,0:T(8,128)S(1)}) custom-call(f32[2,12,8,128]{3,2,1,0:T(8,128)S(1)} %get-tuple-element.32.values_ref.ext_ref, f32[2,64,8,128]{3,2,1,0:T(8,128)S(1)} %get-tuple-element.33.reward_ref, s32[2,64,8,128]{3,2,1,0:T(8,128)S(1)} %get-tuple-element.34.index_ref), custom_call_target="tpu_custom_call" | custom-call | flops 5000000 | bytes 5000000 | tf_op jit(solution)/shard_map/policy/pallas_call | solution.py:804
  54.1 0.2 collective-permute-done.1.other_ref
  54.2 15.2 %push_mass.1 = (f32[512,128]{1,0:T(8,128)S(1)}, f32[512,128]{1,0:T(8,128)S(1)}) custom-call(s32[16]{0:T(128)S(1)} %copy-done.4, f32[2,96,8,128]{3,2,1,0:T(8,128)S(1)} %regroup.3.mine_ref, f32[2,96,8,128]{3,2,1,0:T(8,128)S(1)} %collective-permute-done.1.other_ref, f32[2,72,8,128]{3,2,1,0:T(8,128)S(1)} %regroup.2.mine_ref.graph_mine, ...), custom_call_target="tpu_custom_call" | custom-call | tf_op jit(solution)/shard_map/push_mass/pallas_call | solution.py:823
  69.4 0.4 collective-permute-start.2
  69.8 1.2 %collective-permute-done.2 = f32[512,128]{1,0:T(8,128)S(1)} collective-permute-done((f32[512,128]{1,0:T(8,128)S(1)}, f32[512,128]{1,0:T(8,128)S(1)}, u32[]{:S(2)}, u32[]{:S(2)}) %collective-permute-start.2) | collective-permute-done | bytes 262176 | tf_op jit(solution)/shard_map/ppermute | solution.py:855
  71.0 16.8 %all_to_all.34 = f32[16,32,128]{2,1,0:T(8,128)S(1)} all-to-all(f32[16,32,128]{2,1,0:T(8,128)S(1)} %bitcast.7), channel_id=1, replica_groups=mesh['gx'=4,'gy'=4,'dst'=2] {'gy','gx'}, dimensions={0} | all-to-all | bytes 524288 | tf_op jit(solution)/shard_map/all_to_all | solution.py:851
  87.8 0.1 collective-permute-start.3
  87.9 0.3 multiply_reduce_fusion
  88.3 0.6 broadcast_in_dim.9
  88.9 2.6 %all-to-all-start.3 = ((f32[32,1,32]{2,1,0:T(1,128)}), f32[32,1,32]{2,1,0:T(1,128)S(1)}, u32[]{:S(2)}, u32[]{:S(2)}) async-start(f32[32,1,32]{2,1,0:T(1,128)} %broadcast_in_dim.9), calls=%async_computation.3 | async-start | bytes 32768 | tf_op jit(solution)/shard_map/all_to_all | solution.py:898
  91.6 0.6 sub.7
  92.2 6.5 %all-to-all-done.3 = f32[32,1,32]{2,1,0:T(1,128)S(1)} async-done(((f32[32,1,32]{2,1,0:T(1,128)}), f32[32,1,32]{2,1,0:T(1,128)S(1)}, u32[]{:S(2)}, u32[]{:S(2)}) %all-to-all-start.3) | async-done | bytes 4128 | tf_op jit(solution)/shard_map/all_to_all | solution.py:898
  98.7 0.6 reduce_sum.29
  (20 shorter events, 0.1 us)
Async XLA Ops:
  3.4 8.5 %copy-start.6 = (bf16[32,8,1024]{2,1,0:T(8,128)(2,1)S(1)}, bf16[32,8,1024]{2,1,0:T(8,128)(2,1)}, u32[]{:S(2)}) copy-start(bf16[32,8,1024]{2,1,0:T(8,128)(2,1)} %feature_any.1) | copy-start | bytes 1572868
  3.4 24.7 %all-to-all-start.1 = ((f32[16,72,128]{2,1,0:T(8,128)}), f32[16,72,128]{2,1,0:T(8,128)S(1)}, u32[]{:S(2)}, u32[]{:S(2)}) async-start(f32[16,72,128]{2,1,0:T(8,128)} %bitcast.8), calls=%async_computation.1 | async-start | bytes 1179648 | tf_op jit(solution)/shard_map/all_to_all | solution.py:851
  11.9 0.8 copy-start
  11.9 0.8 copy-start.7
  11.9 0.8 copy-start.3
  11.9 0.8 copy-start.5
  12.7 0.8 copy-start.1
  12.7 0.8 copy-start.2
  28.2 23.2 %all-to-all-start = ((f32[16,96,128]{2,1,0:T(8,128)}), f32[16,96,128]{2,1,0:T(8,128)S(1)}, u32[]{:S(2)}, u32[]{:S(2)}) async-start(f32[16,96,128]{2,1,0:T(8,128)} %bitcast), calls=%async_computation | async-start | bytes 1572864 | tf_op jit(solution)/shard_map/all_to_all | solution.py:851
  32.3 2.2 %copy-start.4 = (s32[16]{0:T(128)S(1)}, s32[16]{0:T(128)}, u32[]{:S(2)}) copy-start(s32[16]{0:T(128)} %dest_ref.3) | copy-start | bytes 196
  32.5 2.1 %collective-permute-start = (f32[2,72,8,128]{3,2,1,0:T(8,128)S(1)}, f32[2,72,8,128]{3,2,1,0:T(8,128)S(1)}, u32[]{:S(2)}, u32[]{:S(2)}) collective-permute-start(f32[2,72,8,128]{3,2,1,0:T(8,128)S(1)} %regroup.2.mine_ref.graph_mine), channel_id=1, source_target_pairs={{0,1},{1,0},{2,3},{3,2},{4,5},{5,4},{6,7},{7,6},{8,9},{9,8},{10,11... | collective-permute-start | bytes 1769480 | tf_op jit(solution)/shard_map/ppermute | solution.py:855
  51.9 2.4 %collective-permute-start.1 = (f32[2,96,8,128]{3,2,1,0:T(8,128)S(1)}, f32[2,96,8,128]{3,2,1,0:T(8,128)S(1)}, u32[]{:S(2)}, u32[]{:S(2)}) collective-permute-start(f32[2,96,8,128]{3,2,1,0:T(8,128)S(1)} %regroup.3.mine_ref), channel_id=1, source_target_pairs={{0,1},{1,0},{2,3},{3,2},{4,5},{5,4},{6,7},{7,6},{8,9},{9,8},{10,11... | collective-permute-start | bytes 2359304 | tf_op jit(solution)/shard_map/ppermute | solution.py:855
  69.4 1.6 %collective-permute-start.2 = (f32[512,128]{1,0:T(8,128)S(1)}, f32[512,128]{1,0:T(8,128)S(1)}, u32[]{:S(2)}, u32[]{:S(2)}) collective-permute-start(f32[512,128]{1,0:T(8,128)S(1)} %get-tuple-element.39), channel_id=1, source_target_pairs={{0,1},{1,0},{2,3},{3,2},{4,5},{5,4},{6,7},{7,6},{8,9},{9,8},{10,11... | collective-permute-start | bytes 786440 | tf_op jit(solution)/shard_map/ppermute | solution.py:855
  87.8 3.7 %collective-permute-start.3 = (f32[32,128]{1,0:T(8,128)S(1)}, f32[32,128]{1,0:T(8,128)S(1)}, u32[]{:S(2)}, u32[]{:S(2)}) collective-permute-start(f32[32,128]{1,0:T(8,128)S(1)} %reduce_sum.27), channel_id=1, source_target_pairs={{0,1},{1,0},{2,3},{3,2},{4,5},{5,4},{6,7},{7,6},{8,9},{9,8},{10,11... | collective-permute-start | bytes 49160 | tf_op jit(solution)/shard_map/ppermute | solution.py:855
  88.9 9.8 %all-to-all-start.3 = ((f32[32,1,32]{2,1,0:T(1,128)}), f32[32,1,32]{2,1,0:T(1,128)S(1)}, u32[]{:S(2)}, u32[]{:S(2)}) async-start(f32[32,1,32]{2,1,0:T(1,128)} %broadcast_in_dim.9), calls=%async_computation.3 | async-start | bytes 32768 | tf_op jit(solution)/shard_map/all_to_all | solution.py:898

commit v2 on v1

--- a/solution.py
+++ b/solution.py
@@ -330,13 +330,15 @@
         out_ref[b * size + edges : (b + 1) * size, :] = jnp.where(first_core, mixed, own)
 
 
-def regroup_kernel(pieces_ref, out_ref):
+def regroup_kernel(pieces_ref, out_ref, padded_ref):
     halves, rows = out_ref.shape[:2]
-    size = pieces_ref.shape[0] // (8 * halves)
+    size, apart = pieces_ref.shape[0] // (8 * halves), padded_ref.shape[0] // (8 * halves)
+    for b in range(8 * halves):
+        padded_ref[b * apart : b * apart + size, :] = pieces_ref[b * size : (b + 1) * size, :]
     for h in range(halves):
 
         def one_row(i, carry, h=h):
-            out_ref[h, i] = of_blocks(pieces_ref, h, i, size)
+            out_ref[h, i] = of_blocks(padded_ref, h, i, apart)
             return carry
 
         lax.fori_loop(0, rows, one_row, 0, unroll=8)
@@ -769,6 +771,9 @@
         out_shape=f32(blocks // 8, pieces.shape[0] // blocks, 8, LANES),
         in_specs=[VMEM_SPEC],
         out_specs=VMEM_SPEC,
+        scratch_shapes=[
+            pltpu.VMEM((blocks * padded_rows(pieces.shape[0] // blocks), LANES), jnp.float32)
+        ],
         compiler_params=PARAMS,
         name="regroup",
     )(pieces)

time: 99.8 us -> 99.5 us (level)
  no operation moved by 1% of the time
where the time goes in v2:
time: 99.5 us; the launch traced here: 99 us
  Pallas kernels  48.6 us (49%)
  blocking collectives  17 us (17%)
  starting transfers between devices  15.9 us (16%)
  waiting for transfers between devices  12.9 us (13%)
  local copies, waits for them, and re-layouts  2.21 us (2%)
  other arithmetic  1.6 us (2%)
    all_to_all x1, blocking collectives, to_blocks(): return lax.all_to_all(array, BLOCK_AXES, 0, 0, tiled=True)  17 us
    pallas_call x1, Pallas kernels, call_values(): pl.pallas_call(functools.partial(value_kernel, grid_x), out_shape=(f32(ha...  16.6 us
    pallas_call x1, Pallas kernels, call_push(): pl.pallas_call(functools.partial(push_kernel, grid_x, scale), out_shape=(...  15 us
    all_to_all x2, starting transfers between devices, to_blocks(): return lax.all_to_all(array, BLOCK_AXES, 0, 0, tiled=True)  12.6 us
    pallas_call x1, Pallas kernels, call_arrange(): pl.pallas_call(arrange_kernel, out_shape=f32(blocks * share, LANES), in_s...  11.7 us
    all_to_all x1, waiting for transfers between devices, per_destination(): terms = lax.all_to_all(terms, (*BLOCK_AXES, 'dst'), 0, 0, tiled=True)  6.47 us
    ppermute x4, waiting for transfers between devices, other_core(): return lax.ppermute(array, 'dst', [(0, 1), (1, 0)])  3.34 us
    all_to_all x2, waiting for transfers between devices, to_blocks(): return lax.all_to_all(array, BLOCK_AXES, 0, 0, tiled=True)  3.06 us
  transfers between devices with their start and end apart: 7, of which 6 were waited for; matrix products, arithmetic and copies ran while one was open for 2% of the time, Pallas kernels for 31%

profile of v2, /device:TPU:0, one launch (start us, length us, event | category | flops | bytes accessed | tf_op | source)
XLA Modules:
  0.0 99.0 jit_solution(10812875959528694741)
XLA Ops:
  0.6 2.8 %own_graph.1 = (f32[1152,128]{1,0:T(8,128)}, f32[8,1024]{1,0:T(8,128)}) custom-call(f32[32]{0:T(128)} %weight_ref.1, bf16[32,8,1024]{2,1,0:T(8,128)(2,1)} %feature_any.1, s32[8,1024]{1,0:T(8,128)} %succ_any.3, s32[8,1024]{1,0:T(8,128)} %valid_any.3, s32[4,128]{1,0:T(4,128)} %border_any.3, f32[16,1024]{1,0:T(8,128)} %anchor_any.3), custom_call_target="tpu_custom_call" | custom-call | tf_op jit(solution)/shard_map/own_graph/pallas_call | solution.py:718
  3.4 0.0 copy-start.6
  3.4 8.5 %all-to-all-start.1 = ((f32[16,72,128]{2,1,0:T(8,128)}), f32[16,72,128]{2,1,0:T(8,128)S(1)}, u32[]{:S(2)}, u32[]{:S(2)}) async-start(f32[16,72,128]{2,1,0:T(8,128)} %bitcast.8), calls=%async_computation.1 | async-start | bytes 1179648 | tf_op jit(solution)/shard_map/all_to_all | solution.py:856
  11.9 0.0 copy-start.3
  11.9 0.1 constant_dynamic-slice_fusion
  12.1 0.6 copy-done
  12.7 0.0 copy-done.7
  12.7 0.0 copy-done.5
  12.7 0.8 copy-done.1
  13.5 11.7 %arrange_turns.1 = f32[1536,128]{1,0:T(8,128)} custom-call(s32[8,1024]{1,0:T(8,128)S(1)} %copy-done.2, s32[8,1024]{1,0:T(8,128)S(1)} %copy-done, s32[4,128]{1,0:T(4,128)S(1)} %copy-done.3, f32[16,1024]{1,0:T(8,128)S(1)} %copy-done.1, f32[8,1024]{1,0:T(8,128)S(1)} %copy-done.5), custom_call_target="tpu_custom_call" | custom-call | flops 4000000000 | bytes 400000 | tf_op jit(solution)/shard_map/arrange_turns/pallas_call | solution.py:742
  25.2 3.0 %all-to-all-done.1 = f32[16,72,128]{2,1,0:T(8,128)S(1)} async-done(((f32[16,72,128]{2,1,0:T(8,128)}), f32[16,72,128]{2,1,0:T(8,128)S(1)}, u32[]{:S(2)}, u32[]{:S(2)}) %all-to-all-start.1) | async-done | bytes 589856 | tf_op jit(solution)/shard_map/all_to_all | solution.py:856
  28.2 4.2 %all-to-all-start = ((f32[16,96,128]{2,1,0:T(8,128)}), f32[16,96,128]{2,1,0:T(8,128)S(1)}, u32[]{:S(2)}, u32[]{:S(2)}) async-start(f32[16,96,128]{2,1,0:T(8,128)} %bitcast), calls=%async_computation | async-start | bytes 1572864 | tf_op jit(solution)/shard_map/all_to_all | solution.py:856
  32.3 0.2 regroup.2.mine_ref.graph_mine
  32.5 0.1 collective-permute-start
  32.6 2.0 %collective-permute-done.other_ref.graph_other = f32[2,72,8,128]{3,2,1,0:T(8,128)S(1)} collective-permute-done((f32[2,72,8,128]{3,2,1,0:T(8,128)S(1)}, f32[2,72,8,128]{3,2,1,0:T(8,128)S(1)}, u32[]{:S(2)}, u32[]{:S(2)}) %collective-permute-start) | collective-permute-done | bytes 589856 | tf_op jit(solution)/shard_map/ppermute | solution.py:860
  34.6 16.6 %soft_values.1 = (f32[2,12,8,128]{3,2,1,0:T(8,128)S(1)}, f32[2,64,8,128]{3,2,1,0:T(8,128)S(1)}, s32[2,64,8,128]{3,2,1,0:T(8,128)S(1)}) custom-call(s32[16]{0:T(128)S(1)} %copy-done.4, f32[2,72,8,128]{3,2,1,0:T(8,128)S(1)} %regroup.2.mine_ref.graph_mine, f32[2,72,8,128]{3,2,1,0:T(8,128)S(1)} %collective-permute-done.other_ref.graph_other), custom_call_target="tpu_custom_call" | custom-call | flops 40000000 | bytes 40000000 | tf_op jit(solution)/shard_map/soft_values/pallas_call | solution.py:786
  51.2 0.1 all-to-all-done
  51.3 0.3 regroup.3.mine_ref
  51.6 0.1 collective-permute-start.1
  51.7 2.1 %policy.1 = (f32[2,64,8,128]{3,2,1,0:T(8,128)S(1)}, f32[2,8,8,128]{3,2,1,0:T(8,128)S(1)}, f32[2,8,8,128]{3,2,1,0:T(8,128)S(1)}) custom-call(f32[2,12,8,128]{3,2,1,0:T(8,128)S(1)} %get-tuple-element.32.values_ref.ext_ref, f32[2,64,8,128]{3,2,1,0:T(8,128)S(1)} %get-tuple-element.33.reward_ref, s32[2,64,8,128]{3,2,1,0:T(8,128)S(1)} %get-tuple-element.34.index_ref), custom_call_target="tpu_custom_call" | custom-call | flops 5000000 | bytes 5000000 | tf_op jit(solution)/shard_map/policy/pallas_call | solution.py:809
  53.8 0.1 collective-permute-done.1.other_ref
  53.9 15.0 %push_mass.1 = (f32[512,128]{1,0:T(8,128)S(1)}, f32[512,128]{1,0:T(8,128)S(1)}) custom-call(s32[16]{0:T(128)S(1)} %copy-done.4, f32[2,96,8,128]{3,2,1,0:T(8,128)S(1)} %regroup.3.mine_ref, f32[2,96,8,128]{3,2,1,0:T(8,128)S(1)} %collective-permute-done.1.other_ref, f32[2,72,8,128]{3,2,1,0:T(8,128)S(1)} %regroup.2.mine_ref.graph_mine, ...), custom_call_target="tpu_custom_call" | custom-call | tf_op jit(solution)/shard_map/push_mass/pallas_call | solution.py:828
  68.9 0.4 collective-permute-start.2
  69.3 1.2 %collective-permute-done.2 = f32[512,128]{1,0:T(8,128)S(1)} collective-permute-done((f32[512,128]{1,0:T(8,128)S(1)}, f32[512,128]{1,0:T(8,128)S(1)}, u32[]{:S(2)}, u32[]{:S(2)}) %collective-permute-start.2) | collective-permute-done | bytes 262176 | tf_op jit(solution)/shard_map/ppermute | solution.py:860
  70.6 17.0 %all_to_all.34 = f32[16,32,128]{2,1,0:T(8,128)S(1)} all-to-all(f32[16,32,128]{2,1,0:T(8,128)S(1)} %bitcast.7), channel_id=1, replica_groups=mesh['gx'=4,'gy'=4,'dst'=2] {'gy','gx'}, dimensions={0} | all-to-all | bytes 524288 | tf_op jit(solution)/shard_map/all_to_all | solution.py:856
  87.6 0.1 collective-permute-start.3
  87.7 0.3 multiply_reduce_fusion
  88.0 0.6 broadcast_in_dim.9
  88.7 2.6 %all-to-all-start.3 = ((f32[32,1,32]{2,1,0:T(1,128)}), f32[32,1,32]{2,1,0:T(1,128)S(1)}, u32[]{:S(2)}, u32[]{:S(2)}) async-start(f32[32,1,32]{2,1,0:T(1,128)} %broadcast_in_dim.9), calls=%async_computation.3 | async-start | bytes 32768 | tf_op jit(solution)/shard_map/all_to_all | solution.py:903
  91.3 0.6 sub.7
  92.0 6.5 %all-to-all-done.3 = f32[32,1,32]{2,1,0:T(1,128)S(1)} async-done(((f32[32,1,32]{2,1,0:T(1,128)}), f32[32,1,32]{2,1,0:T(1,128)S(1)}, u32[]{:S(2)}, u32[]{:S(2)}) %all-to-all-start.3) | async-done | bytes 4128 | tf_op jit(solution)/shard_map/all_to_all | solution.py:903
  98.4 0.6 reduce_sum.29
  (20 shorter events, 0.1 us)
Async XLA Ops:
  3.4 8.5 %copy-start.6 = (bf16[32,8,1024]{2,1,0:T(8,128)(2,1)S(1)}, bf16[32,8,1024]{2,1,0:T(8,128)(2,1)}, u32[]{:S(2)}) copy-start(bf16[32,8,1024]{2,1,0:T(8,128)(2,1)} %feature_any.1) | copy-start | bytes 1572868
  3.4 24.7 %all-to-all-start.1 = ((f32[16,72,128]{2,1,0:T(8,128)}), f32[16,72,128]{2,1,0:T(8,128)S(1)}, u32[]{:S(2)}, u32[]{:S(2)}) async-start(f32[16,72,128]{2,1,0:T(8,128)} %bitcast.8), calls=%async_computation.1 | async-start | bytes 1179648 | tf_op jit(solution)/shard_map/all_to_all | solution.py:856
  11.9 0.8 copy-start
  11.9 0.8 copy-start.7
  11.9 0.8 copy-start.3
  11.9 0.8 copy-start.5
  12.7 0.8 copy-start.1
  12.7 0.8 copy-start.2
  28.2 23.2 %all-to-all-start = ((f32[16,96,128]{2,1,0:T(8,128)}), f32[16,96,128]{2,1,0:T(8,128)S(1)}, u32[]{:S(2)}, u32[]{:S(2)}) async-start(f32[16,96,128]{2,1,0:T(8,128)} %bitcast), calls=%async_computation | async-start | bytes 1572864 | tf_op jit(solution)/shard_map/all_to_all | solution.py:856
  32.3 2.3 %copy-start.4 = (s32[16]{0:T(128)S(1)}, s32[16]{0:T(128)}, u32[]{:S(2)}) copy-start(s32[16]{0:T(128)} %dest_ref.3) | copy-start | bytes 196
  32.5 2.1 %collective-permute-start = (f32[2,72,8,128]{3,2,1,0:T(8,128)S(1)}, f32[2,72,8,128]{3,2,1,0:T(8,128)S(1)}, u32[]{:S(2)}, u32[]{:S(2)}) collective-permute-start(f32[2,72,8,128]{3,2,1,0:T(8,128)S(1)} %regroup.2.mine_ref.graph_mine), channel_id=1, source_target_pairs={{0,1},{1,0},{2,3},{3,2},{4,5},{5,4},{6,7},{7,6},{8,9},{9,8},{10,11... | collective-permute-start | bytes 1769480 | tf_op jit(solution)/shard_map/ppermute | solution.py:860
  51.6 2.4 %collective-permute-start.1 = (f32[2,96,8,128]{3,2,1,0:T(8,128)S(1)}, f32[2,96,8,128]{3,2,1,0:T(8,128)S(1)}, u32[]{:S(2)}, u32[]{:S(2)}) collective-permute-start(f32[2,96,8,128]{3,2,1,0:T(8,128)S(1)} %regroup.3.mine_ref), channel_id=1, source_target_pairs={{0,1},{1,0},{2,3},{3,2},{4,5},{5,4},{6,7},{7,6},{8,9},{9,8},{10,11... | collective-permute-start | bytes 2359304 | tf_op jit(solution)/shard_map/ppermute | solution.py:860
  68.9 1.6 %collective-permute-start.2 = (f32[512,128]{1,0:T(8,128)S(1)}, f32[512,128]{1,0:T(8,128)S(1)}, u32[]{:S(2)}, u32[]{:S(2)}) collective-permute-start(f32[512,128]{1,0:T(8,128)S(1)} %get-tuple-element.39), channel_id=1, source_target_pairs={{0,1},{1,0},{2,3},{3,2},{4,5},{5,4},{6,7},{7,6},{8,9},{9,8},{10,11... | collective-permute-start | bytes 786440 | tf_op jit(solution)/shard_map/ppermute | solution.py:860
  87.6 3.7 %collective-permute-start.3 = (f32[32,128]{1,0:T(8,128)S(1)}, f32[32,128]{1,0:T(8,128)S(1)}, u32[]{:S(2)}, u32[]{:S(2)}) collective-permute-start(f32[32,128]{1,0:T(8,128)S(1)} %reduce_sum.27), channel_id=1, source_target_pairs={{0,1},{1,0},{2,3},{3,2},{4,5},{5,4},{6,7},{7,6},{8,9},{9,8},{10,11... | collective-permute-start | bytes 49160 | tf_op jit(solution)/shard_map/ppermute | solution.py:860
  88.7 9.8 %all-to-all-start.3 = ((f32[32,1,32]{2,1,0:T(1,128)}), f32[32,1,32]{2,1,0:T(1,128)S(1)}, u32[]{:S(2)}, u32[]{:S(2)}) async-start(f32[32,1,32]{2,1,0:T(1,128)} %broadcast_in_dim.9), calls=%async_computation.3 | async-start | bytes 32768 | tf_op jit(solution)/shard_map/all_to_all | solution.py:903

commit v3 on v2

--- a/solution.py
+++ b/solution.py
@@ -465,7 +465,8 @@
         backup(ext_ref, spare_ref)
         return carry
 
-    lax.fori_loop(0, (HORIZON - 2) // 2, two_backups, 0)
+    for step in range((HORIZON - 2) // 2):
+        two_backups(step, 0)
     backup(spare_ref, ext_ref)
     bring_halo(ext_ref)
 

time: 99.5 us -> 99.6 us (level)
  transfers between devices with their start and end apart: 7 -> 7, of which waited for: 6 -> 5; matrix products, arithmetic and copies ran while one was open for 2% -> 2% of each run, Pallas kernels for 31% -> 31%
where the time goes in v3:
time: 99.6 us; the launch traced here: 99.1 us
  Pallas kernels  48.7 us (49%)
  blocking collectives  17.1 us (17%)
  starting transfers between devices  16 us (16%)
  waiting for transfers between devices  12.7 us (13%)
  local copies, waits for them, and re-layouts  2.21 us (2%)
  other arithmetic  1.6 us (2%)
    all_to_all x1, blocking collectives, to_blocks(): return lax.all_to_all(array, BLOCK_AXES, 0, 0, tiled=True)  17.1 us
    pallas_call x1, Pallas kernels, call_values(): pl.pallas_call(functools.partial(value_kernel, grid_x), out_shape=(f32(ha...  16.7 us
    pallas_call x1, Pallas kernels, call_push(): pl.pallas_call(functools.partial(push_kernel, grid_x, scale), out_shape=(...  15 us
    all_to_all x2, starting transfers between devices, to_blocks(): return lax.all_to_all(array, BLOCK_AXES, 0, 0, tiled=True)  12.6 us
    pallas_call x1, Pallas kernels, call_arrange(): pl.pallas_call(arrange_kernel, out_shape=f32(blocks * share, LANES), in_s...  11.7 us
    all_to_all x1, waiting for transfers between devices, per_destination(): terms = lax.all_to_all(terms, (*BLOCK_AXES, 'dst'), 0, 0, tiled=True)  6.47 us
    ppermute x4, waiting for transfers between devices, other_core(): return lax.ppermute(array, 'dst', [(0, 1), (1, 0)])  3.26 us
    all_to_all x2, waiting for transfers between devices, to_blocks(): return lax.all_to_all(array, BLOCK_AXES, 0, 0, tiled=True)  2.96 us
  transfers between devices with their start and end apart: 7, of which 5 were waited for; matrix products, arithmetic and copies ran while one was open for 2% of the time, Pallas kernels for 31%

profile of v3, /device:TPU:0, one launch (start us, length us, event | category | flops | bytes accessed | tf_op | source)
XLA Modules:
  0.0 99.1 jit_solution(4607669496326925026)
XLA Ops:
  0.6 2.8 %own_graph.1 = (f32[1152,128]{1,0:T(8,128)}, f32[8,1024]{1,0:T(8,128)}) custom-call(f32[32]{0:T(128)} %weight_ref.1, bf16[32,8,1024]{2,1,0:T(8,128)(2,1)} %feature_any.1, s32[8,1024]{1,0:T(8,128)} %succ_any.3, s32[8,1024]{1,0:T(8,128)} %valid_any.3, s32[4,128]{1,0:T(4,128)} %border_any.3, f32[16,1024]{1,0:T(8,128)} %anchor_any.3), custom_call_target="tpu_custom_call" | custom-call | tf_op jit(solution)/shard_map/own_graph/pallas_call | solution.py:719
  3.4 0.0 copy-start.6
  3.4 8.5 %all-to-all-start.1 = ((f32[16,72,128]{2,1,0:T(8,128)}), f32[16,72,128]{2,1,0:T(8,128)S(1)}, u32[]{:S(2)}, u32[]{:S(2)}) async-start(f32[16,72,128]{2,1,0:T(8,128)} %bitcast.8), calls=%async_computation.1 | async-start | bytes 1179648 | tf_op jit(solution)/shard_map/all_to_all | solution.py:857
  11.9 0.0 copy-start.3
  11.9 0.0 copy-start.5
  11.9 0.1 constant_dynamic-slice_fusion
  12.1 0.6 copy-done
  12.7 0.0 copy-done.7
  12.7 0.0 copy-done.5
  12.7 0.8 copy-done.1
  13.5 11.7 %arrange_turns.1 = f32[1536,128]{1,0:T(8,128)} custom-call(s32[8,1024]{1,0:T(8,128)S(1)} %copy-done.2, s32[8,1024]{1,0:T(8,128)S(1)} %copy-done, s32[4,128]{1,0:T(4,128)S(1)} %copy-done.3, f32[16,1024]{1,0:T(8,128)S(1)} %copy-done.1, f32[8,1024]{1,0:T(8,128)S(1)} %copy-done.5), custom_call_target="tpu_custom_call" | custom-call | flops 4000000000 | bytes 400000 | tf_op jit(solution)/shard_map/arrange_turns/pallas_call | solution.py:743
  25.2 3.0 %all-to-all-done.1 = f32[16,72,128]{2,1,0:T(8,128)S(1)} async-done(((f32[16,72,128]{2,1,0:T(8,128)}), f32[16,72,128]{2,1,0:T(8,128)S(1)}, u32[]{:S(2)}, u32[]{:S(2)}) %all-to-all-start.1) | async-done | bytes 589856 | tf_op jit(solution)/shard_map/all_to_all | solution.py:857
  28.2 4.2 %all-to-all-start = ((f32[16,96,128]{2,1,0:T(8,128)}), f32[16,96,128]{2,1,0:T(8,128)S(1)}, u32[]{:S(2)}, u32[]{:S(2)}) async-start(f32[16,96,128]{2,1,0:T(8,128)} %bitcast), calls=%async_computation | async-start | bytes 1572864 | tf_op jit(solution)/shard_map/all_to_all | solution.py:857
  32.3 0.2 regroup.2.mine_ref.graph_mine
  32.5 0.1 collective-permute-start
  32.6 2.0 %collective-permute-done.other_ref.graph_other = f32[2,72,8,128]{3,2,1,0:T(8,128)S(1)} collective-permute-done((f32[2,72,8,128]{3,2,1,0:T(8,128)S(1)}, f32[2,72,8,128]{3,2,1,0:T(8,128)S(1)}, u32[]{:S(2)}, u32[]{:S(2)}) %collective-permute-start) | collective-permute-done | bytes 589856 | tf_op jit(solution)/shard_map/ppermute | solution.py:861
  34.6 16.7 %soft_values.1 = (f32[2,12,8,128]{3,2,1,0:T(8,128)S(1)}, f32[2,64,8,128]{3,2,1,0:T(8,128)S(1)}, s32[2,64,8,128]{3,2,1,0:T(8,128)S(1)}) custom-call(s32[16]{0:T(128)S(1)} %copy-done.4, f32[2,72,8,128]{3,2,1,0:T(8,128)S(1)} %regroup.2.mine_ref.graph_mine, f32[2,72,8,128]{3,2,1,0:T(8,128)S(1)} %collective-permute-done.other_ref.graph_other), custom_call_target="tpu_custom_call" | custom-call | flops 40000000 | bytes 40000000 | tf_op jit(solution)/shard_map/soft_values/pallas_call | solution.py:787
  51.3 0.3 regroup.3.mine_ref
  51.6 0.2 collective-permute-start.1
  51.8 2.1 %policy.1 = (f32[2,64,8,128]{3,2,1,0:T(8,128)S(1)}, f32[2,8,8,128]{3,2,1,0:T(8,128)S(1)}, f32[2,8,8,128]{3,2,1,0:T(8,128)S(1)}) custom-call(f32[2,12,8,128]{3,2,1,0:T(8,128)S(1)} %get-tuple-element.32.values_ref.ext_ref, f32[2,64,8,128]{3,2,1,0:T(8,128)S(1)} %get-tuple-element.33.reward_ref, s32[2,64,8,128]{3,2,1,0:T(8,128)S(1)} %get-tuple-element.34.index_ref), custom_call_target="tpu_custom_call" | custom-call | flops 5000000 | bytes 5000000 | tf_op jit(solution)/shard_map/policy/pallas_call | solution.py:810
  53.9 0.1 collective-permute-done.1.other_ref
  54.0 15.0 %push_mass.1 = (f32[512,128]{1,0:T(8,128)S(1)}, f32[512,128]{1,0:T(8,128)S(1)}) custom-call(s32[16]{0:T(128)S(1)} %copy-done.4, f32[2,96,8,128]{3,2,1,0:T(8,128)S(1)} %regroup.3.mine_ref, f32[2,96,8,128]{3,2,1,0:T(8,128)S(1)} %collective-permute-done.1.other_ref, f32[2,72,8,128]{3,2,1,0:T(8,128)S(1)} %regroup.2.mine_ref.graph_mine, ...), custom_call_target="tpu_custom_call" | custom-call | tf_op jit(solution)/shard_map/push_mass/pallas_call | solution.py:829
  69.0 0.4 collective-permute-start.2
  69.4 1.2 %collective-permute-done.2 = f32[512,128]{1,0:T(8,128)S(1)} collective-permute-done((f32[512,128]{1,0:T(8,128)S(1)}, f32[512,128]{1,0:T(8,128)S(1)}, u32[]{:S(2)}, u32[]{:S(2)}) %collective-permute-start.2) | collective-permute-done | bytes 262176 | tf_op jit(solution)/shard_map/ppermute | solution.py:861
  70.6 17.1 %all_to_all.34 = f32[16,32,128]{2,1,0:T(8,128)S(1)} all-to-all(f32[16,32,128]{2,1,0:T(8,128)S(1)} %bitcast.7), channel_id=1, replica_groups=mesh['gx'=4,'gy'=4,'dst'=2] {'gy','gx'}, dimensions={0} | all-to-all | bytes 524288 | tf_op jit(solution)/shard_map/all_to_all | solution.py:857
  87.7 0.1 collective-permute-start.3
  87.8 0.3 multiply_reduce_fusion
  88.1 0.6 broadcast_in_dim.9
  88.7 2.6 %all-to-all-start.3 = ((f32[32,1,32]{2,1,0:T(1,128)}), f32[32,1,32]{2,1,0:T(1,128)S(1)}, u32[]{:S(2)}, u32[]{:S(2)}) async-start(f32[32,1,32]{2,1,0:T(1,128)} %broadcast_in_dim.9), calls=%async_computation.3 | async-start | bytes 32768 | tf_op jit(solution)/shard_map/all_to_all | solution.py:904
  91.4 0.6 sub.7
  92.1 6.5 %all-to-all-done.3 = f32[32,1,32]{2,1,0:T(1,128)S(1)} async-done(((f32[32,1,32]{2,1,0:T(1,128)}), f32[32,1,32]{2,1,0:T(1,128)S(1)}, u32[]{:S(2)}, u32[]{:S(2)}) %all-to-all-start.3) | async-done | bytes 4128 | tf_op jit(solution)/shard_map/all_to_all | solution.py:904
  98.5 0.6 reduce_sum.29
  (20 shorter events, 0.1 us)
Async XLA Ops:
  3.4 8.5 %copy-start.6 = (bf16[32,8,1024]{2,1,0:T(8,128)(2,1)S(1)}, bf16[32,8,1024]{2,1,0:T(8,128)(2,1)}, u32[]{:S(2)}) copy-start(bf16[32,8,1024]{2,1,0:T(8,128)(2,1)} %feature_any.1) | copy-start | bytes 1572868
  3.4 24.7 %all-to-all-start.1 = ((f32[16,72,128]{2,1,0:T(8,128)}), f32[16,72,128]{2,1,0:T(8,128)S(1)}, u32[]{:S(2)}, u32[]{:S(2)}) async-start(f32[16,72,128]{2,1,0:T(8,128)} %bitcast.8), calls=%async_computation.1 | async-start | bytes 1179648 | tf_op jit(solution)/shard_map/all_to_all | solution.py:857
  11.9 0.8 copy-start
  11.9 0.8 copy-start.7
  11.9 0.8 copy-start.3
  11.9 0.8 copy-start.5
  12.7 0.8 copy-start.1
  12.7 0.8 copy-start.2
  28.2 23.2 %all-to-all-start = ((f32[16,96,128]{2,1,0:T(8,128)}), f32[16,96,128]{2,1,0:T(8,128)S(1)}, u32[]{:S(2)}, u32[]{:S(2)}) async-start(f32[16,96,128]{2,1,0:T(8,128)} %bitcast), calls=%async_computation | async-start | bytes 1572864 | tf_op jit(solution)/shard_map/all_to_all | solution.py:857
  32.3 2.3 %copy-start.4 = (s32[16]{0:T(128)S(1)}, s32[16]{0:T(128)}, u32[]{:S(2)}) copy-start(s32[16]{0:T(128)} %dest_ref.3) | copy-start | bytes 196
  32.5 2.1 %collective-permute-start = (f32[2,72,8,128]{3,2,1,0:T(8,128)S(1)}, f32[2,72,8,128]{3,2,1,0:T(8,128)S(1)}, u32[]{:S(2)}, u32[]{:S(2)}) collective-permute-start(f32[2,72,8,128]{3,2,1,0:T(8,128)S(1)} %regroup.2.mine_ref.graph_mine), channel_id=1, source_target_pairs={{0,1},{1,0},{2,3},{3,2},{4,5},{5,4},{6,7},{7,6},{8,9},{9,8},{10,11... | collective-permute-start | bytes 1769480 | tf_op jit(solution)/shard_map/ppermute | solution.py:861
  51.6 2.4 %collective-permute-start.1 = (f32[2,96,8,128]{3,2,1,0:T(8,128)S(1)}, f32[2,96,8,128]{3,2,1,0:T(8,128)S(1)}, u32[]{:S(2)}, u32[]{:S(2)}) collective-permute-start(f32[2,96,8,128]{3,2,1,0:T(8,128)S(1)} %regroup.3.mine_ref), channel_id=1, source_target_pairs={{0,1},{1,0},{2,3},{3,2},{4,5},{5,4},{6,7},{7,6},{8,9},{9,8},{10,11... | collective-permute-start | bytes 2359304 | tf_op jit(solution)/shard_map/ppermute | solution.py:861
  69.0 1.6 %collective-permute-start.2 = (f32[512,128]{1,0:T(8,128)S(1)}, f32[512,128]{1,0:T(8,128)S(1)}, u32[]{:S(2)}, u32[]{:S(2)}) collective-permute-start(f32[512,128]{1,0:T(8,128)S(1)} %get-tuple-element.39), channel_id=1, source_target_pairs={{0,1},{1,0},{2,3},{3,2},{4,5},{5,4},{6,7},{7,6},{8,9},{9,8},{10,11... | collective-permute-start | bytes 786440 | tf_op jit(solution)/shard_map/ppermute | solution.py:861
  87.7 3.7 %collective-permute-start.3 = (f32[32,128]{1,0:T(8,128)S(1)}, f32[32,128]{1,0:T(8,128)S(1)}, u32[]{:S(2)}, u32[]{:S(2)}) collective-permute-start(f32[32,128]{1,0:T(8,128)S(1)} %reduce_sum.27), channel_id=1, source_target_pairs={{0,1},{1,0},{2,3},{3,2},{4,5},{5,4},{6,7},{7,6},{8,9},{9,8},{10,11... | collective-permute-start | bytes 49160 | tf_op jit(solution)/shard_map/ppermute | solution.py:861
  88.7 9.8 %all-to-all-start.3 = ((f32[32,1,32]{2,1,0:T(1,128)}), f32[32,1,32]{2,1,0:T(1,128)S(1)}, u32[]{:S(2)}, u32[]{:S(2)}) async-start(f32[32,1,32]{2,1,0:T(1,128)} %broadcast_in_dim.9), calls=%async_computation.3 | async-start | bytes 32768 | tf_op jit(solution)/shard_map/all_to_all | solution.py:904
